TPU v7x, 32 devices: a whole 2x2x4 slice. The times are simulated.
32 devices in a mesh: grp: 2 (over y), beam: 8 (over z, x), gy: 2 (over core).
Axes of the slice: x: 2, y: 2, z: 4, core: 2. Of those that a mesh axis runs over, the one named last changes fastest.
Arguments:
- concentration: float32 [16, 32, 16, 256], P('grp', 'beam', None, 'gy'), parts along dimension 0, may hold values from 0.2 to 2
- incident_mu: float32 [8], replicated, may hold values from 0.003125 to 0.03125
- exit_mu: float32 [3, 8], replicated, may hold values from 0.000390625 to 0.00390625
- line_element: int32 [3], replicated, may hold values from 0 to 7
- tilt_index: int32 [1], replicated, may hold values from 0 to 63
- shear: int32 [32], P('grp'), parts along dimension 0, may hold values from 0 to 15
- data: float32 [128, 3, 16, 256], P('grp', None, None, 'gy'), parts along dimension 0, may hold values from 1.6 to 16
Outputs:
- updated: float32 [16, 32, 16, 256], P('grp', 'beam', None, 'gy'), parts along dimension 0
There are 2 independent parts, one for each index of `grp`. A program takes and returns all parts, laid end to end along the dimension named above; an argument that names none is the same for every part. Nothing has to cross between parts.
All inputs are finite; a program needn't handle non-finite values.
Results may differ from a plain program's by a relative error of at most 0.000067.
Values sent between devices are 32-bit elements; how exact they have to be, the bound alone decides.
A program may use at most 64 MiB of HBM per device.

v0:
```python
import jax
import jax.numpy as jnp
from jax import lax
from jax.sharding import PartitionSpec as P

blend_weight = 0.05


def carried_in(part, axis, combine, identity):
    count = lax.axis_size(axis)
    place = lax.axis_index(axis)
    ahead = count - 1 - place
    gathered = lax.all_gather(part, axis)
    state = jnp.zeros_like(part) + jnp.asarray(identity, part.dtype)

    def one(step, state):
        source = count - 1 - step
        return combine(state, lax.dynamic_index_in_dim(gathered, source, 0, False))

    return lax.fori_loop(0, ahead, one, state)


def add_up(earlier, later):
    return earlier + later


def per_device(concentration, incident_mu, exit_mu, line_element, tilt_index, shear, data):
    elements, cells_beam, slices, cells_y = concentration.shape
    start_cell = lax.axis_index("beam") * cells_beam
    beam_cells = start_cell + jnp.arange(cells_beam, dtype=jnp.int32)
    support = (beam_cells[:, None] >= shear[None, :]).astype(jnp.float32)
    live_cells = concentration * support[None, :, :, None]
    incident_rate = jnp.einsum(
        "e,ebzy->bzy", incident_mu, live_cells, precision=lax.Precision.HIGHEST
    )
    local_sum = jnp.cumsum(incident_rate, axis=0)
    totals = local_sum[-1]
    all_totals = lax.all_gather(totals[None], "beam", axis=0, tiled=True)
    below_mask = (jnp.arange(all_totals.shape[0], dtype=jnp.int32) < lax.axis_index("beam")).astype(
        jnp.float32
    )
    before = jnp.einsum("n,nzy->zy", below_mask, all_totals, precision=lax.Precision.HIGHEST)
    incident = jnp.exp(-(before[None] + local_sum - 0.5 * incident_rate))
    exit_rate = jnp.einsum("le,ebzy->lbzy", exit_mu, live_cells, precision=lax.Precision.HIGHEST)
    suffix = jnp.flip(jnp.cumsum(jnp.flip(exit_rate, 3), axis=3), 3)
    slab_totals = suffix[:, :, :, 0]
    after_sum = carried_in(slab_totals, "gy", add_up, jnp.zeros_like(slab_totals))
    exit_path = after_sum[:, :, :, None] + suffix - 0.5 * exit_rate
    weight = incident[None] * jnp.exp(-exit_path)
    onehot = (line_element[:, None] == jnp.arange(elements, dtype=jnp.int32)[None, :]).astype(
        jnp.float32
    )
    source = jnp.einsum("le,ebzy->lbzy", onehot, live_cells, precision=lax.Precision.HIGHEST)
    partial_value = jnp.sum(weight * source, axis=1)
    measured = lax.dynamic_index_in_dim(data, tilt_index[0], 0, keepdims=False)
    emission = lax.psum(partial_value, "beam")
    ratios = measured / emission
    kept_weight = weight * support[None, :, :, None]
    numerator = blend_weight + jnp.einsum(
        "le,lbzy->ebzy", onehot, kept_weight * ratios[:, None], precision=lax.Precision.HIGHEST
    )
    denominator = blend_weight + jnp.einsum(
        "le,lbzy->ebzy", onehot, kept_weight, precision=lax.Precision.HIGHEST
    )
    return concentration * numerator / denominator


def solution(mesh):
    placed = (
        P("grp", "beam", None, "gy"),
        P(),
        P(),
        P(),
        P(),
        P("grp"),
        P("grp", None, None, "gy"),
    )
    return jax.shard_map(
        per_device,
        mesh=mesh,
        in_specs=placed,
        out_specs=P("grp", "beam", None, "gy"),
        check_vma=False,
    )
```

profile of v0, /device:TPU:0, one launch (start us, length us, event | category | flops | bytes accessed | tf_op | source)
XLA Modules:
  0.0 83.0 jit_solution(7655232553926409823)
XLA Ops:
  0.0 0.8 %compare_convert_fusion = f32[4,16]{1,0:T(4,128)S(1)} fusion(s32[16]{0:T(128)} %param.14, s32[4]{0:T(128)S(1)} %iota_add_fusion), kind=kLoop, calls=%fused_computation.29 | loop fusion | flops 128 | bytes 336 | tf_op jit(solution)/shard_map/convert_element_type | solution.py:31
  0.8 1.0 %broadcast_multiply_fusion = f32[8,4,16,128]{3,2,1,0:T(8,128)S(1)} fusion(f32[8,4,16,128]{3,2,1,0:T(8,128)} %param.9, f32[4,16]{1,0:T(4,128)S(1)} %compare_convert_fusion), kind=kLoop, calls=%fused_computation.14 | loop fusion | flops 65536 | bytes 524544 | tf_op jit(solution)/shard_map/mul | solution.py:32
  1.9 1.2 %fusion.4 = f32[1,4,16,128]{3,0,2,1:T(1,128)S(1)} fusion(f32[8,4,16,128]{3,2,1,0:T(8,128)S(1)} %broadcast_multiply_fusion, f32[8]{0:T(128)} %param.10), kind=kOutput, calls=%fused_computation.9 | convolution fusion | flops 786432 | bytes 294944 | tf_op jit(solution)/shard_map/e,ebzy->bzy/dot_general | solution.py:33
  3.1 0.0 copy-start.2
  3.1 0.1 fusion.25
  3.2 32.3 %all_gather.6 = f32[8,16,128]{2,1,0:T(8,128)S(1)} all-gather(f32[1,16,128]{2,1,0:T(8,128)S(1)} %slice.9), channel_id=1, replica_groups=mesh['grp'=2,'beam'=8,'gy'=2] {'beam'}, dimensions={0}, use_global_device_ids=true | all-gather | bytes 73728 | tf_op jit(solution)/shard_map/all_gather | solution.py:38
  35.5 0.2 fusion.10
  35.7 1.2 %convolution_bitcast_fusion = f32[3,4,16,128]{3,0,2,1:T(4,128)S(1)} fusion(f32[8,4,16,128]{3,2,1,0:T(8,128)S(1)} %broadcast_multiply_fusion, f32[3,8]{1,0:T(4,128)} %param.11), kind=kOutput, calls=%fused_computation.6 | convolution fusion | flops 2359296 | bytes 360544 | tf_op jit(solution)/shard_map/le,ebzy->lbzy/dot_general | solution.py:44
  36.9 0.2 rev.7
  37.1 0.0 copy-start.1
  37.1 3.4 %reduce_window_sum.23 = f32[3,4,16,128]{3,2,1,0:T(8,128)S(1)} reduce-window(f32[3,4,16,128]{3,2,1,0:T(8,128)S(1)} %copy.22, f32[]{:T(128)} %constant.46.clone.1), window={size=1x1x1x128 pad=0_0x0_0x0_0x127_0}, to_apply=%region_1.2 | reduce-window | flops 3121152 | bytes 196612 | tf_op jit(solution)/shard_map/jit(cumsum)/reduce_window_sum | solution.py:45
  40.5 0.1 slice.10
  40.6 0.1 copy.23
  40.7 1.8 %all-gather = f32[6,4,16,1]{2,1,3,0:T(4,128)S(1)} all-gather(f32[3,4,16,1]{2,1,3,0:T(4,128)S(1)} %copy.23), channel_id=2, replica_groups=mesh['grp'=2,'beam'=8,'gy'=2] {'gy'}, dimensions={0}, use_global_device_ids=true | all-gather | bytes 2304 | tf_op jit(solution)/shard_map/all_gather | solution.py:13
  42.6 0.1 copy.24
  42.7 0.1 copy.25
  42.8 0.2 rev.8
  43.0 0.1 exponential_multiply_fusion
  43.1 0.4 fusion.2
  43.6 37.0 %psum.7 = f32[3,16,128]{2,0,1:T(4,128)S(1)} all-reduce(f32[3,16,128]{2,0,1:T(4,128)S(1)} %fusion.2), channel_id=1, replica_groups=mesh['grp'=2,'beam'=8,'gy'=2] {'beam'}, use_global_device_ids=true, to_apply=%region_5.6 | all-reduce | flops 6144 | bytes 49152 | tf_op jit(solution)/shard_map/psum | solution.py:56
  81.3 0.0 copy-done
  81.3 0.4 convolution_add_fusion
  81.7 0.5 fusion.1
  82.2 0.8 copy.29
  (12 shorter events, 0.1 us)
Async XLA Ops:
  0.0 81.3 %copy-start = (f32[64,3,16,128]{3,2,1,0:T(8,128)S(1)}, f32[64,3,16,128]{3,2,1,0:T(8,128)}, u32[]{:S(2)}) copy-start(f32[64,3,16,128]{3,2,1,0:T(8,128)} %param.15) | copy-start | bytes 4718596
  3.1 40.1 %copy-start.2 = (s32[3]{0:T(128)S(1)}, s32[3]{0:T(128)}, u32[]{:S(2)}) copy-start(s32[3]{0:T(128)} %param.12) | copy-start | bytes 40
  37.1 44.6 %copy-start.1 = (f32[8,4,16,128]{3,2,1,0:T(8,128)S(1)}, f32[8,4,16,128]{3,2,1,0:T(8,128)}, u32[]{:S(2)}) copy-start(f32[8,4,16,128]{3,2,1,0:T(8,128)} %param.9) | copy-start | bytes 786436
where the time goes:
time: 83.2 us; the launch traced here: 83 us
  blocking collectives  71.2 us (86%)
  other arithmetic  5.6 us (7%)
  matrix products  3.83 us (5%)
  local copies, waits for them, and re-layouts  1.55 us (2%)
    psum x1, blocking collectives, per_device(): emission = lax.psum(partial_value, 'beam')  37 us
    all_gather x1, blocking collectives, per_device(): all_totals = lax.all_gather(totals[None], 'beam', axis=0, tiled=True)  32.3 us
    another operation x1, other arithmetic, per_device(): suffix = jnp.flip(jnp.cumsum(jnp.flip(exit_rate, 3), axis=3), 3)  3.42 us
    all_gather x1, blocking collectives, carried_in(): gathered = lax.all_gather(part, axis)  1.82 us

commit v1 on v0

v1 whole, which is shorter than its diff:
```python
import functools

import jax
import jax.numpy as jnp
from jax import lax
from jax.experimental import pallas as pl
from jax.experimental.pallas import tpu as pltpu
from jax.sharding import PartitionSpec as P

blend_weight = 0.05
MESH = pl.DeviceIdType.MESH


def loop(count, body):
    if count <= 16:
        for step in range(count):
            body(step)
    else:

        def one(step, carry):
            body(step)
            return carry

        lax.fori_loop(0, count, one, 0)


def fold(count, body, carry):
    if count <= 16:
        for step in range(count):
            carry = body(step, carry)
        return carry
    return lax.fori_loop(0, count, body, carry)


def layout(slices, bricks, lines):
    owners = min(slices, bricks)
    while slices % owners or bricks % owners:
        owners -= 1
    chunk = slices // owners
    rows = -(-(lines + 1) * chunk // 8) * 8
    return owners, bricks // owners, chunk, rows


def kernel(
    bricks,
    slabs,
    conc_hbm,
    incident_hbm,
    exit_hbm,
    line_hbm,
    tilt_hbm,
    shear_hbm,
    data_hbm,
    factor,
    conc,
    data,
    incident_mu,
    exit_mu,
    line,
    tilt,
    shear,
    weight,
    slab_out,
    slab_in,
    sent,
    taken,
    reply,
    back,
    measured,
    load_sem,
    slab_send,
    slab_recv,
    out_send,
    out_recv,
    back_send,
    back_recv,
):
    elements, cells, slices, width = conc.shape
    lines = exit_mu.shape[0]
    owners, stride, chunk, rows = layout(slices, bricks, lines)
    me = lax.axis_index("beam")
    slab = lax.axis_index("gy")
    rank = me if stride == 1 else me // stride
    is_owner = True if stride == 1 else lax.rem(me, stride) == 0

    loads = [
        pltpu.make_async_copy(src, dst, load_sem.at[k])
        for k, (src, dst) in enumerate(
            (
                (conc_hbm, conc),
                (exit_hbm, exit_mu),
                (shear_hbm, shear),
                (incident_hbm, incident_mu),
                (line_hbm, line),
                (tilt_hbm, tilt),
                (data_hbm, data),
            )
        )
    ]
    for load in loads:
        load.start()

    def when(condition, body):
        if condition is True:
            body()
        else:
            pl.when(condition)(body)

    def other_bricks(body):
        if bricks <= 16:
            for k in range(1, bricks):
                body(lax.rem(me + k, bricks))
        else:
            loop(bricks, lambda s: pl.when(s != me)(lambda: body(s)))

    def other_owners(body):
        if stride == 1:
            other_bricks(lambda s: body(s, s))
        else:
            loop(owners, lambda j: pl.when(j * stride != me)(lambda: body(j, j * stride)))

    barrier = pltpu.get_barrier_semaphore()

    def greet_brick(s):
        pl.semaphore_signal(barrier, inc=1, device_id={"beam": s}, device_id_type=MESH)

    def greet_owner(j, s):
        greet_brick(s)

    for d in range(1, slabs):
        pl.semaphore_signal(
            barrier,
            inc=1,
            device_id={"gy": lax.rem(slab + d, slabs)},
            device_id_type=MESH,
        )
    if stride == 1:
        other_bricks(greet_brick)
    else:
        pl.when(is_owner)(lambda: other_bricks(greet_brick))
        pl.when(jnp.logical_not(is_owner))(lambda: other_owners(greet_owner))

    def side(shape, axis):
        return lax.broadcasted_iota(jnp.int32, shape, axis)

    square = (2 * width, 2 * width)
    row = lax.rem(side(square, 0), width)
    column = side(square, 1)
    sums = jnp.where(
        column >= width, 1.0, jnp.where(row > column, 1.0, jnp.where(row == column, 0.5, 0.0))
    ).astype(jnp.bfloat16)

    tile = (slices, width)
    z_of = side(tile, 0)
    lane = side(tile, 1)
    for load in loads[:-1]:
        load.wait()
    first = jnp.zeros(tile, jnp.int32)
    for z in range(slices):
        first = jnp.where(z_of == z, shear[z], first)
    support = [
        jnp.where(me * cells + b >= first, 1.0, 0.0).astype(jnp.float32) for b in range(cells)
    ]
    exit_rate = []
    for l in range(lines):
        for b in range(cells):
            total = conc[0, b] * exit_mu[l, 0]
            for e in range(1, elements):
                total += conc[e, b] * exit_mu[l, e]
            exit_rate.append(total * support[b])
    stacked = jnp.concatenate(exit_rate, axis=0)
    high = stacked.astype(jnp.bfloat16)
    low = (stacked - high.astype(jnp.float32)).astype(jnp.bfloat16)
    paths = jnp.dot(
        jnp.concatenate([high, low], axis=1), sums, preferred_element_type=jnp.float32
    )

    packed = jnp.zeros(tile, jnp.float32)
    for c in range(lines * cells):
        packed = jnp.where(lane == c, paths[c * slices : (c + 1) * slices, width:], packed)
    slab_out[...] = packed

    def slab_copy(d, target):
        return pltpu.make_async_remote_copy(
            src_ref=slab_out,
            dst_ref=slab_in.at[d - 1],
            send_sem=slab_send.at[d - 1],
            recv_sem=slab_recv.at[d - 1],
            device_id={"gy": target},
            device_id_type=MESH,
        )

    if stride == 1:
        pl.semaphore_wait(barrier, bricks - 1 + slabs - 1)
    else:
        pl.when(is_owner)(lambda: pl.semaphore_wait(barrier, bricks - 1 + slabs - 1))
        pl.when(jnp.logical_not(is_owner))(
            lambda: pl.semaphore_wait(barrier, owners + slabs - 1)
        )
    for d in range(1, slabs):
        pl.when(slab >= d)(lambda d=d: slab_copy(d, slab - d).start())

    before = jnp.zeros(tile, jnp.float32)
    for b in range(cells):
        rate = conc[0, b] * incident_mu[0]
        for e in range(1, elements):
            rate += conc[e, b] * incident_mu[e]
        rate *= support[b]
        depth = before + 0.5 * rate
        before += rate
        for l in range(lines):
            c = l * cells + b
            path = paths[c * slices : (c + 1) * slices, :width]
            weight[c] = support[b] * jnp.exp(-(depth + path))

    def put(q, value):
        for i in range(chunk):
            sent[pl.ds(q * chunk + i, owners, stride=rows), :] = value[
                i * owners : (i + 1) * owners
            ]

    put(0, before)
    if rows > (lines + 1) * chunk:
        for r in range((lines + 1) * chunk, rows):
            sent[pl.ds(r, owners, stride=rows), :] = jnp.zeros((owners, width), jnp.float32)

    for d in range(1, slabs):

        @pl.when(slab + d < slabs)
        def _(d=d):
            slab_copy(d, slab - d).wait_recv()
            passed = jnp.exp(-slab_in[d - 1])
            for c in range(lines * cells):
                weight[c] *= jnp.broadcast_to(passed[:, c : c + 1], tile)

    for l in range(lines):
        source = line[l]
        partial = weight[l * cells] * conc[source, 0]
        for b in range(1, cells):
            partial += weight[l * cells + b] * conc[source, b]
        put(l + 1, partial)

    def part(j):
        return pl.ds(pl.multiple_of(j * rows, 8), rows)

    def out_copy(j, target, source):
        return pltpu.make_async_remote_copy(
            src_ref=sent.at[part(j)],
            dst_ref=taken.at[source],
            send_sem=out_send.at[j],
            recv_sem=out_recv.at[source],
            device_id={"beam": target},
            device_id_type=MESH,
        )

    def back_copy(j, target):
        return pltpu.make_async_remote_copy(
            src_ref=reply.at[target],
            dst_ref=back.at[part(j)],
            send_sem=back_send.at[target],
            recv_sem=back_recv.at[j],
            device_id={"beam": target},
            device_id_type=MESH,
        )

    other_owners(lambda j, s: out_copy(j, s, me).start())

    loads[-1].wait()
    for j in range(1):
        for l in range(lines):
            values = data[tilt[0], l]
            for i in range(chunk):
                measured[pl.ds((l + 1) * chunk + i, owners, stride=rows), :] = values[
                    i * owners : (i + 1) * owners
                ]
    for r in list(range(chunk)) + list(range((lines + 1) * chunk, rows)):
        measured[pl.ds(r, owners, stride=rows), :] = jnp.zeros((owners, width), jnp.float32)

    def own():
        taken[me] = sent[part(rank), :]
        other_bricks(lambda s: out_copy(rank, s, s).wait_recv())
        head = side((rows, width), 0) < chunk

        def one(s, carry):
            run, emission = carry
            start = jnp.where(head, run, 0.0)
            spread = start
            for q in range(1, lines + 1):
                spread += pltpu.roll(start, q * chunk, 0)
            passed = jnp.exp(-spread)
            reply[s] = passed
            values = taken[s]
            return run + values, emission + passed * values

        zero = jnp.zeros((rows, width), jnp.float32)
        _, emission = fold(bricks, one, (zero, zero))
        ratio = measured[part(rank), :] / emission

        def finish(s):
            reply[s] = jnp.where(head, reply[s], ratio)

        loop(bricks, finish)
        other_bricks(lambda s: back_copy(rank, s).start())
        back[part(rank), :] = reply[me]

    when(is_owner, own)
    other_owners(lambda j, s: back_copy(j, me).wait_recv())

    def get(q):
        return jnp.concatenate(
            [back[pl.ds(q * chunk + i, owners, stride=rows), :] for i in range(chunk)], axis=0
        )

    arrived = get(0)
    ratios = [get(l + 1) for l in range(lines)]
    same = [
        [jnp.where(line[l] == line[k], 1.0, 0.0).astype(jnp.float32) for k in range(lines)]
        for l in range(lines)
    ]
    for b in range(cells):
        kept = [weight[l * cells + b] * arrived for l in range(lines)]
        raised = [kept[l] * ratios[l] for l in range(lines)]
        for l in range(lines):
            top = blend_weight + raised[l]
            bottom = blend_weight + kept[l]
            for k in range(lines):
                if k != l:
                    top += same[l][k] * raised[k]
                    bottom += same[l][k] * kept[k]
            factor[l, b] = top / bottom

    other_owners(lambda j, s: out_copy(j, s, me).wait_send())
    when(is_owner, lambda: other_bricks(lambda s: back_copy(rank, s).wait_send()))
    for d in range(1, slabs):
        pl.when(slab >= d)(lambda d=d: slab_copy(d, slab - d).wait_send())


def per_device(
    bricks, slabs, concentration, incident_mu, exit_mu, line_element, tilt_index, shear, data
):
    elements, cells, slices, width = concentration.shape
    lines = exit_mu.shape[0]
    owners, _, _, rows = layout(slices, bricks, lines)
    f32 = jnp.float32
    factor = pl.pallas_call(
        functools.partial(kernel, bricks, slabs),
        out_shape=jax.ShapeDtypeStruct((lines, cells, slices, width), f32),
        in_specs=[pl.BlockSpec(memory_space=pl.ANY)] * 7,
        out_specs=pl.BlockSpec(memory_space=pltpu.VMEM),
        scratch_shapes=[
            pltpu.VMEM(concentration.shape, f32),
            pltpu.VMEM(data.shape, f32),
            pltpu.SMEM(incident_mu.shape, f32),
            pltpu.SMEM(exit_mu.shape, f32),
            pltpu.SMEM(line_element.shape, jnp.int32),
            pltpu.SMEM(tilt_index.shape, jnp.int32),
            pltpu.SMEM(shear.shape, jnp.int32),
            pltpu.VMEM((lines * cells, slices, width), f32),
            pltpu.VMEM((slices, width), f32),
            pltpu.VMEM((max(slabs - 1, 1), slices, width), f32),
            pltpu.VMEM((owners * rows, width), f32),
            pltpu.VMEM((bricks, rows, width), f32),
            pltpu.VMEM((bricks, rows, width), f32),
            pltpu.VMEM((owners * rows, width), f32),
            pltpu.VMEM((owners * rows, width), f32),
            pltpu.SemaphoreType.DMA((7,)),
            pltpu.SemaphoreType.DMA((max(slabs - 1, 1),)),
            pltpu.SemaphoreType.DMA((max(slabs - 1, 1),)),
            pltpu.SemaphoreType.DMA((owners,)),
            pltpu.SemaphoreType.DMA((bricks,)),
            pltpu.SemaphoreType.DMA((bricks,)),
            pltpu.SemaphoreType.DMA((owners,)),
        ],
        compiler_params=pltpu.CompilerParams(
            collective_id=0, has_side_effects=True, vmem_limit_bytes=16 * 1024 * 1024
        ),
        name="update_factor",
    )(concentration, incident_mu, exit_mu, line_element, tilt_index, shear, data)
    element = lax.broadcasted_iota(jnp.int32, concentration.shape, 0)
    scale = jnp.ones_like(concentration)
    for l in range(lines):
        scale = jnp.where(element == line_element[l], factor[l][None], scale)
    return concentration * scale


def solution(mesh):
    placed = (
        P("grp", "beam", None, "gy"),
        P(),
        P(),
        P(),
        P(),
        P("grp"),
        P("grp", None, None, "gy"),
    )
    return jax.shard_map(
        functools.partial(per_device, mesh.shape["beam"], mesh.shape["gy"]),
        mesh=mesh,
        in_specs=placed,
        out_specs=P("grp", "beam", None, "gy"),
        check_vma=False,
    )
```

time: 83.2 us -> 25.2 us (0.30)
  blocking collectives: 71.2 us -> 0 us
  Pallas kernels: 0 us -> 15.1 us
  local copies, waits for them, and re-layouts: 1.55 us -> 6.41 us
  matrix products: 3.83 us -> 0 us
  other arithmetic: 5.6 us -> 2.78 us
    psum x1 -> x0, blocking collectives: 37 us -> none  [per_device(): emission = lax.psum(partial_value, 'beam')]
    all_gather x2 -> x0, blocking collectives: 34.1 us -> none  [the longest x1 32.3 us: per_device(): all_totals = lax.all_gather(totals[None], 'beam', axis=0, tiled=True)]
    pallas_call x0 -> x1, Pallas kernels: none -> 15.1 us  [per_device(): pl.pallas_call(functools.partial(kernel, bricks, slabs), out_shape=jax.Sh...]
    unnamed x6 -> x12, local copies, waits for them, and re-layouts: 0.02 us -> 5 us
    dot_general x6 -> x0, matrix products: 3.83 us -> none  [the longest x1 1.19 us: per_device(): jnp.einsum('le,ebzy->lbzy', exit_mu, live_cells, precision=lax.Precision....]
    another operation x2 -> x0, other arithmetic: 3.52 us -> none  [the longest x1 3.42 us: per_device(): suffix = jnp.flip(jnp.cumsum(jnp.flip(exit_rate, 3), axis=3), 3)]
    eq x0 -> x2, other arithmetic: none -> 1.96 us  [per_device(): scale = jnp.where(element == line_element[l], factor[l][None], scale)]
    slice x3 -> x1, local copies, waits for them, and re-layouts: 0.22 us -> 1.4 us  [per_device(): scale = jnp.where(element == line_element[l], factor[l][None], scale)]
where the time goes in v1:
time: 25.2 us; the launch traced here: 24.9 us
  Pallas kernels  15.1 us (60%)
  local copies, waits for them, and re-layouts  6.41 us (25%)
  other arithmetic  2.78 us (11%)
  between operations  0.7 us (3%)
    pallas_call x1, Pallas kernels, per_device(): pl.pallas_call(functools.partial(kernel, bricks, slabs), out_shape=jax.Sh...  15.1 us
    unnamed x12, local copies, waits for them, and re-layouts  5 us
    eq x2, other arithmetic, per_device(): scale = jnp.where(element == line_element[l], factor[l][None], scale)  1.96 us
    slice x1, local copies, waits for them, and re-layouts, per_device(): scale = jnp.where(element == line_element[l], factor[l][None], scale)  1.4 us
    mul x1, other arithmetic, per_device(): return concentration * scale  0.82 us

profile of v1, /device:TPU:0, one launch (start us, length us, event | category | flops | bytes accessed | tf_op | source)
XLA Modules:
  0.0 24.9 jit_solution(15398066046748518195)
XLA Ops:
  0.7 1.4 %fusion = (s32[1]{0:T(128)}, s32[1]{0:T(128)}, s32[1]{0:T(128)}) fusion(s32[3]{0:T(128)} %line_hbm.1), kind=kLoop, calls=%fused_computation.7 | loop fusion | bytes 24 | tf_op jit(solution)/shard_map/slice | solution.py:382
  2.1 0.6 %iota_compare_fusion.2 = pred[8]{0:T(512)(128)(4,1)S(1)} fusion(s32[]{:T(128)} %bitcast), kind=kLoop, calls=%fused_computation.6 | loop fusion | flops 8 | bytes 12 | tf_op jit(solution)/shard_map/eq | solution.py:382
  2.7 1.3 %iota_compare_fusion = (pred[8]{0:T(512)(128)(4,1)S(1)}, pred[8]{0:T(512)(128)(4,1)S(1)}) fusion(s32[]{:T(128)} %bitcast.4, s32[]{:T(128)} %bitcast.2), kind=kLoop, calls=%fused_computation.4 | loop fusion | flops 16 | bytes 24 | tf_op jit(solution)/shard_map/eq | solution.py:382
  4.0 0.0 copy-start
  4.0 1.4 %copy-done = f32[64,3,16,128]{3,2,1,0:T(8,128)S(1)} copy-done((f32[64,3,16,128]{3,2,1,0:T(8,128)S(1)}, f32[64,3,16,128]{3,2,1,0:T(8,128)}, u32[]{:S(2)}) %copy-start) | copy-done | bytes 1572888
  5.4 0.0 copy-start.1
  5.4 0.9 %copy-done.1 = f32[8,4,16,128]{3,2,1,0:T(8,128)S(1)} copy-done((f32[8,4,16,128]{3,2,1,0:T(8,128)S(1)}, f32[8,4,16,128]{3,2,1,0:T(8,128)}, u32[]{:S(2)}) %copy-start.1) | copy-done | bytes 262168
  6.4 0.0 copy-start.2
  6.4 0.7 %copy-done.2 = s32[3]{0:T(128)S(1)} copy-done((s32[3]{0:T(128)S(1)}, s32[3]{0:T(128)}, u32[]{:S(2)}) %copy-start.2) | copy-done | bytes 36
  7.0 0.0 copy-start.3
  7.0 0.7 %copy-done.3 = f32[3,8]{1,0:T(4,128)S(1)} copy-done((f32[3,8]{1,0:T(4,128)S(1)}, f32[3,8]{1,0:T(4,128)}, u32[]{:S(2)}) %copy-start.3) | copy-done | bytes 120
  7.7 0.0 copy-start.4
  7.7 0.7 %copy-done.4 = f32[8]{0:T(128)S(1)} copy-done((f32[8]{0:T(128)S(1)}, f32[8]{0:T(128)}, u32[]{:S(2)}) %copy-start.4) | copy-done | bytes 56
  8.4 0.0 copy-start.5
  8.4 0.7 %copy-done.5 = s32[16]{0:T(128)S(1)} copy-done((s32[16]{0:T(128)S(1)}, s32[16]{0:T(128)}, u32[]{:S(2)}) %copy-start.5) | copy-done | bytes 88
  9.0 15.1 %update_factor.1 = f32[3,4,16,128]{3,2,1,0:T(8,128)S(1)} custom-call(f32[8,4,16,128]{3,2,1,0:T(8,128)S(1)} %copy-done.1, f32[8]{0:T(128)S(1)} %copy-done.4, f32[3,8]{1,0:T(4,128)S(1)} %copy-done.3, s32[3]{0:T(128)S(1)} %copy-done.2, s32[1]{0:T(128)S(6)} %copy.8.tilt_hbm, s32[16]{0:T(128)S(1)} %copy-done.5, f32[64,3,16,128]{3,2,1,0:T(8,128)S(1)} %copy-done), custom_call_target="tpu_custom_call" | custom-call | tf_op jit(solution)/shard_map/update_factor/pallas_call | solution.py:345
  24.1 0.8 %select_multiply_fusion = f32[8,4,16,128]{3,2,1,0:T(8,128)} fusion(f32[8,4,16,128]{3,2,1,0:T(8,128)S(1)} %copy-done.1, f32[4,16,128]{2,1,0:T(8,128)S(1)} %get-tuple-element.6, f32[4,16,128]{2,1,0:T(8,128)S(1)} %get-tuple-element.7, f32[4,16,128]{2,1,0:T(8,128)S(1)} %get-tuple-element.5, pred[8]{0:T(512)(128)(4,1)S(1)} %get-tuple-element.11, ...), kind=kLoop, calls=%fused_computation | loop fusion | flops 262144 | bytes 622616 | tf_op jit(solution)/shard_map/mul | solution.py:383
  (1 shorter events, 0.0 us)
Async XLA Ops:
  4.0 1.4 %copy-start = (f32[64,3,16,128]{3,2,1,0:T(8,128)S(1)}, f32[64,3,16,128]{3,2,1,0:T(8,128)}, u32[]{:S(2)}) copy-start(f32[64,3,16,128]{3,2,1,0:T(8,128)} %data_hbm.1) | copy-start | bytes 4718596
  5.4 0.9 %copy-start.1 = (f32[8,4,16,128]{3,2,1,0:T(8,128)S(1)}, f32[8,4,16,128]{3,2,1,0:T(8,128)}, u32[]{:S(2)}) copy-start(f32[8,4,16,128]{3,2,1,0:T(8,128)} %conc_hbm.1) | copy-start | bytes 786436
  6.4 0.7 %copy-start.2 = (s32[3]{0:T(128)S(1)}, s32[3]{0:T(128)}, u32[]{:S(2)}) copy-start(s32[3]{0:T(128)} %line_hbm.1) | copy-start | bytes 40
  7.0 0.7 %copy-start.3 = (f32[3,8]{1,0:T(4,128)S(1)}, f32[3,8]{1,0:T(4,128)}, u32[]{:S(2)}) copy-start(f32[3,8]{1,0:T(4,128)} %exit_hbm.1) | copy-start | bytes 292
  7.7 0.7 %copy-start.4 = (f32[8]{0:T(128)S(1)}, f32[8]{0:T(128)}, u32[]{:S(2)}) copy-start(f32[8]{0:T(128)} %incident_hbm.1) | copy-start | bytes 100
  8.4 0.7 %copy-start.5 = (s32[16]{0:T(128)S(1)}, s32[16]{0:T(128)}, u32[]{:S(2)}) copy-start(s32[16]{0:T(128)} %shear_hbm.1) | copy-start | bytes 196

commit v2 on v1

--- a/solution.py
+++ b/solution.py
@@ -51,7 +51,7 @@
     tilt_hbm,
     shear_hbm,
     data_hbm,
-    factor,
+    updated,
     conc,
     data,
     incident_mu,
@@ -266,13 +266,12 @@
     other_owners(lambda j, s: out_copy(j, s, me).start())
 
     loads[-1].wait()
-    for j in range(1):
-        for l in range(lines):
-            values = data[tilt[0], l]
-            for i in range(chunk):
-                measured[pl.ds((l + 1) * chunk + i, owners, stride=rows), :] = values[
-                    i * owners : (i + 1) * owners
-                ]
+    for l in range(lines):
+        values = data[tilt[0], l]
+        for i in range(chunk):
+            measured[pl.ds((l + 1) * chunk + i, owners, stride=rows), :] = values[
+                i * owners : (i + 1) * owners
+            ]
     for r in list(range(chunk)) + list(range((lines + 1) * chunk, rows)):
         measured[pl.ds(r, owners, stride=rows), :] = jnp.zeros((owners, width), jnp.float32)
 
@@ -320,6 +319,7 @@
     for b in range(cells):
         kept = [weight[l * cells + b] * arrived for l in range(lines)]
         raised = [kept[l] * ratios[l] for l in range(lines)]
+        factor = []
         for l in range(lines):
             top = blend_weight + raised[l]
             bottom = blend_weight + kept[l]
@@ -327,7 +327,12 @@
                 if k != l:
                     top += same[l][k] * raised[k]
                     bottom += same[l][k] * kept[k]
-            factor[l, b] = top / bottom
+            factor.append(top / bottom)
+        for e in range(elements):
+            scale = 1.0
+            for l in range(lines):
+                scale = jnp.where(line[l] == e, factor[l], scale)
+            updated[e, b] = conc[e, b] * scale
 
     other_owners(lambda j, s: out_copy(j, s, me).wait_send())
     when(is_owner, lambda: other_bricks(lambda s: back_copy(rank, s).wait_send()))
@@ -342,9 +347,10 @@
     lines = exit_mu.shape[0]
     owners, _, _, rows = layout(slices, bricks, lines)
     f32 = jnp.float32
-    factor = pl.pallas_call(
+    arguments = (concentration, incident_mu, exit_mu, line_element, tilt_index, shear, data)
+    return pl.pallas_call(
         functools.partial(kernel, bricks, slabs),
-        out_shape=jax.ShapeDtypeStruct((lines, cells, slices, width), f32),
+        out_shape=pltpu.VMEM(concentration.shape, f32),
         in_specs=[pl.BlockSpec(memory_space=pl.ANY)] * 7,
         out_specs=pl.BlockSpec(memory_space=pltpu.VMEM),
         scratch_shapes=[
@@ -374,13 +380,8 @@
         compiler_params=pltpu.CompilerParams(
             collective_id=0, has_side_effects=True, vmem_limit_bytes=16 * 1024 * 1024
         ),
-        name="update_factor",
-    )(concentration, incident_mu, exit_mu, line_element, tilt_index, shear, data)
-    element = lax.broadcasted_iota(jnp.int32, concentration.shape, 0)
-    scale = jnp.ones_like(concentration)
-    for l in range(lines):
-        scale = jnp.where(element == line_element[l], factor[l][None], scale)
-    return concentration * scale
+        name="update",
+    )(*(x if x.size == 1 else pltpu.with_memory_space_constraint(x, pltpu.HBM) for x in arguments))
 
 
 def solution(mesh):

time: 25.2 us -> 16.6 us (0.66)
  local copies, waits for them, and re-layouts: 6.41 us -> 0.71 us
  other arithmetic: 2.78 us -> 0 us
    unnamed x12 -> x1, local copies, waits for them, and re-layouts: 5 us -> 0.71 us
    eq x2 -> x0, other arithmetic: 1.96 us -> none  [per_device(): scale = jnp.where(element == line_element[l], factor[l][None], scale)]
    slice x1 -> x0, local copies, waits for them, and re-layouts: 1.4 us -> none  [per_device(): scale = jnp.where(element == line_element[l], factor[l][None], scale)]
    mul x1 -> x0, other arithmetic: 0.82 us -> none  [per_device(): return concentration * scale]
where the time goes in v2:
time: 16.6 us; the launch traced here: 16.4 us
  Pallas kernels  15.1 us (91%)
  local copies, waits for them, and re-layouts  0.71 us (4%)
  between operations  0.66 us (4%)
    pallas_call x1, Pallas kernels, per_device(): pl.pallas_call(functools.partial(kernel, bricks, slabs), out_shape=pltpu....  15.1 us
    unnamed x1, local copies, waits for them, and re-layouts  0.71 us

profile of v2, /device:TPU:0, one launch (start us, length us, event | category | flops | bytes accessed | tf_op | source)
XLA Modules:
  0.0 16.4 jit_solution(5338162761049912969)
XLA Ops:
  0.7 15.1 %update.1 = f32[8,4,16,128]{3,2,1,0:T(8,128)S(1)} custom-call(f32[8,4,16,128]{3,2,1,0:T(8,128)} %conc_hbm.1, f32[8]{0:T(128)} %incident_hbm.1, f32[3,8]{1,0:T(4,128)} %exit_hbm.1, s32[3]{0:T(128)} %line_hbm.1, s32[1]{0:T(128)S(6)} %copy.10.tilt_hbm, s32[16]{0:T(128)} %shear_hbm.1, f32[64,3,16,128]{3,2,1,0:T(8,128)} %data_hbm.1), custom_call_target="tpu_custom_call" | custom-call | tf_op jit(solution)/shard_map/update/pallas_call | solution.py:351
  15.7 0.7 %copy.9 = f32[8,4,16,128]{3,2,1,0:T(8,128)} copy(f32[8,4,16,128]{3,2,1,0:T(8,128)S(1)} %update.1) | data formatting | bytes 524288

commit v3 on v2

--- a/solution.py
+++ b/solution.py
@@ -62,6 +62,8 @@
     weight,
     slab_out,
     slab_in,
+    near_out,
+    near_in,
     sent,
     taken,
     reply,
@@ -70,6 +72,8 @@
     load_sem,
     slab_send,
     slab_recv,
+    near_send,
+    near_recv,
     out_send,
     out_recv,
     back_send,
@@ -127,18 +131,36 @@
     def greet_owner(j, s):
         greet_brick(s)
 
-    for d in range(1, slabs):
-        pl.semaphore_signal(
-            barrier,
-            inc=1,
-            device_id={"gy": lax.rem(slab + d, slabs)},
-            device_id_type=MESH,
-        )
-    if stride == 1:
+    def greet_later(brick):
+        for d in range(1, slabs):
+
+            @pl.when(slab + d < slabs)
+            def _(d=d):
+                pl.semaphore_signal(
+                    barrier,
+                    inc=1,
+                    device_id={"beam": brick, "gy": slab + d},
+                    device_id_type=MESH,
+                )
+
+    def greet_as_owner():
         other_bricks(greet_brick)
-    else:
-        pl.when(is_owner)(lambda: other_bricks(greet_brick))
-        pl.when(jnp.logical_not(is_owner))(lambda: other_owners(greet_owner))
+        loop(bricks, greet_later)
+
+    def greet_as_other():
+        other_owners(greet_owner)
+        greet_later(me)
+
+    when(is_owner, greet_as_owner)
+    if stride > 1:
+        pl.when(jnp.logical_not(is_owner))(greet_as_other)
+
+    def wait_barrier():
+        when(is_owner, lambda: pl.semaphore_wait(barrier, bricks - 1 + slab * owners))
+        if stride > 1:
+            pl.when(jnp.logical_not(is_owner))(
+                lambda: pl.semaphore_wait(barrier, owners + slab * (owners + 1))
+            )
 
     def side(shape, axis):
         return lax.broadcasted_iota(jnp.int32, shape, axis)
@@ -175,10 +197,17 @@
         jnp.concatenate([high, low], axis=1), sums, preferred_element_type=jnp.float32
     )
 
-    packed = jnp.zeros(tile, jnp.float32)
-    for c in range(lines * cells):
-        packed = jnp.where(lane == c, paths[c * slices : (c + 1) * slices, width:], packed)
-    slab_out[...] = packed
+    span = cells * rows
+    used = (lines + 1) * chunk
+
+    def part(j):
+        return pl.ds(pl.multiple_of(j * rows, 8), rows)
+
+    def put(target, step, q, value):
+        for i in range(chunk):
+            target[pl.ds(q * chunk + i, owners, stride=step), :] = value[
+                i * owners : (i + 1) * owners
+            ]
 
     def slab_copy(d, target):
         return pltpu.make_async_remote_copy(
@@ -186,67 +215,25 @@
             dst_ref=slab_in.at[d - 1],
             send_sem=slab_send.at[d - 1],
             recv_sem=slab_recv.at[d - 1],
-            device_id={"gy": target},
+            device_id={"beam": me, "gy": target},
             device_id_type=MESH,
         )
 
-    if stride == 1:
-        pl.semaphore_wait(barrier, bricks - 1 + slabs - 1)
-    else:
-        pl.when(is_owner)(lambda: pl.semaphore_wait(barrier, bricks - 1 + slabs - 1))
-        pl.when(jnp.logical_not(is_owner))(
-            lambda: pl.semaphore_wait(barrier, owners + slabs - 1)
+    def near_copy(d, j, target, source):
+        return pltpu.make_async_remote_copy(
+            src_ref=near_out.at[part(j)],
+            dst_ref=near_in.at[d - 1, source],
+            send_sem=near_send.at[d - 1, j],
+            recv_sem=near_recv.at[d - 1, source],
+            device_id={"beam": j * stride, "gy": target},
+            device_id_type=MESH,
         )
-    for d in range(1, slabs):
-        pl.when(slab >= d)(lambda d=d: slab_copy(d, slab - d).start())
-
-    before = jnp.zeros(tile, jnp.float32)
-    for b in range(cells):
-        rate = conc[0, b] * incident_mu[0]
-        for e in range(1, elements):
-            rate += conc[e, b] * incident_mu[e]
-        rate *= support[b]
-        depth = before + 0.5 * rate
-        before += rate
-        for l in range(lines):
-            c = l * cells + b
-            path = paths[c * slices : (c + 1) * slices, :width]
-            weight[c] = support[b] * jnp.exp(-(depth + path))
-
-    def put(q, value):
-        for i in range(chunk):
-            sent[pl.ds(q * chunk + i, owners, stride=rows), :] = value[
-                i * owners : (i + 1) * owners
-            ]
-
-    put(0, before)
-    if rows > (lines + 1) * chunk:
-        for r in range((lines + 1) * chunk, rows):
-            sent[pl.ds(r, owners, stride=rows), :] = jnp.zeros((owners, width), jnp.float32)
-
-    for d in range(1, slabs):
-
-        @pl.when(slab + d < slabs)
-        def _(d=d):
-            slab_copy(d, slab - d).wait_recv()
-            passed = jnp.exp(-slab_in[d - 1])
-            for c in range(lines * cells):
-                weight[c] *= jnp.broadcast_to(passed[:, c : c + 1], tile)
-
-    for l in range(lines):
-        source = line[l]
-        partial = weight[l * cells] * conc[source, 0]
-        for b in range(1, cells):
-            partial += weight[l * cells + b] * conc[source, b]
-        put(l + 1, partial)
-
-    def part(j):
-        return pl.ds(pl.multiple_of(j * rows, 8), rows)
-
-    def out_copy(j, target, source):
+
+    def out_copy(j, target, source, tiles):
+        size = tiles * rows
         return pltpu.make_async_remote_copy(
-            src_ref=sent.at[part(j)],
-            dst_ref=taken.at[source],
+            src_ref=sent.at[pl.ds(pl.multiple_of(j * span, 8), size)],
+            dst_ref=taken.at[source, pl.ds(0, size)],
             send_sem=out_send.at[j],
             recv_sem=out_recv.at[source],
             device_id={"beam": target},
@@ -263,7 +250,70 @@
             device_id_type=MESH,
         )
 
-    other_owners(lambda j, s: out_copy(j, s, me).start())
+    @pl.when(slab > 0)
+    def _():
+        put(near_out, rows, 0, jnp.ones(tile, jnp.float32))
+        for r in range(used, rows):
+            near_out[pl.ds(r, owners, stride=rows), :] = jnp.zeros((owners, width), jnp.float32)
+        for l in range(lines):
+            packed = jnp.zeros(tile, jnp.float32)
+            for b in range(cells):
+                c = l * cells + b
+                packed = jnp.where(lane == b, paths[c * slices : (c + 1) * slices, width:], packed)
+            passed = jnp.exp(-packed)
+            slab_out[l] = passed
+            put(near_out, rows, l + 1, passed)
+        wait_barrier()
+        for d in range(1, slabs):
+
+            @pl.when(slab >= d)
+            def _(d=d):
+                loop(owners, lambda j: near_copy(d, j, slab - d, me).start())
+                slab_copy(d, slab - d).start()
+
+    before = jnp.zeros(tile, jnp.float32)
+    rates = []
+    for b in range(cells):
+        rate = conc[0, b] * incident_mu[0]
+        for e in range(1, elements):
+            rate += conc[e, b] * incident_mu[e]
+        rate *= support[b]
+        rates.append(rate)
+        depth = before + 0.5 * rate
+        before += rate
+        for l in range(lines):
+            c = l * cells + b
+            path = paths[c * slices : (c + 1) * slices, :width]
+            weight[c] = support[b] * jnp.exp(-(depth + path))
+
+    for b in range(cells):
+        for r in range(used, rows):
+            sent[pl.ds(b * rows + r, owners, stride=span), :] = jnp.zeros(
+                (owners, width), jnp.float32
+            )
+
+    @pl.when(slab < slabs - 1)
+    def _():
+        for b in range(cells):
+            tiles = sent.at[pl.ds(b * rows, owners * span - b * rows)]
+            put(tiles, span, 0, rates[b])
+            for l in range(lines):
+                put(tiles, span, l + 1, weight[l * cells + b] * conc[line[l], b])
+
+        pl.when(slab == 0)(wait_barrier)
+        other_owners(lambda j, s: out_copy(j, s, me, cells).start())
+
+    @pl.when(slab == slabs - 1)
+    def _():
+        put(sent, span, 0, before)
+        for l in range(lines):
+            partial = weight[l * cells] * conc[line[l], 0]
+            for b in range(1, cells):
+                partial += weight[l * cells + b] * conc[line[l], b]
+            put(sent, span, l + 1, partial)
+        if slabs == 1:
+            wait_barrier()
+        other_owners(lambda j, s: out_copy(j, s, me, 1).start())
 
     loads[-1].wait()
     for l in range(lines):
@@ -276,8 +326,40 @@
         measured[pl.ds(r, owners, stride=rows), :] = jnp.zeros((owners, width), jnp.float32)
 
     def own():
-        taken[me] = sent[part(rank), :]
-        other_bricks(lambda s: out_copy(rank, s, s).wait_recv())
+        taken[me, 0:rows] = sent[pl.ds(pl.multiple_of(rank * span, 8), rows), :]
+
+        @pl.when(slab < slabs - 1)
+        def _():
+            taken[me] = sent[pl.ds(pl.multiple_of(rank * span, 8), span), :]
+            for d in range(1, slabs):
+
+                @pl.when(slab + d < slabs)
+                def _(d=d):
+                    loop(bricks, lambda s: near_copy(d, rank, slab, s).wait_recv())
+
+            other_bricks(lambda s: out_copy(rank, s, s, cells).wait_recv())
+
+            def reduce(s):
+                for d in range(1, slabs):
+
+                    @pl.when(slab + d < slabs)
+                    def _(d=d):
+                        passed = near_in[d - 1, s]
+                        for b in range(cells):
+                            at = pl.ds(b * rows, rows)
+                            taken[s, at] *= jnp.broadcast_to(passed[:, b : b + 1], (rows, width))
+
+                total = taken[s, 0:rows]
+                for b in range(1, cells):
+                    total += taken[s, b * rows : (b + 1) * rows]
+                taken[s, 0:rows] = total
+
+            loop(bricks, reduce)
+
+        @pl.when(slab == slabs - 1)
+        def _():
+            other_bricks(lambda s: out_copy(rank, s, s, 1).wait_recv())
+
         head = side((rows, width), 0) < chunk
 
         def one(s, carry):
@@ -288,7 +370,7 @@
                 spread += pltpu.roll(start, q * chunk, 0)
             passed = jnp.exp(-spread)
             reply[s] = passed
-            values = taken[s]
+            values = taken[s, 0:rows]
             return run + values, emission + passed * values
 
         zero = jnp.zeros((rows, width), jnp.float32)
@@ -303,6 +385,17 @@
         back[part(rank), :] = reply[me]
 
     when(is_owner, own)
+    for d in range(1, slabs):
+
+        @pl.when(slab + d < slabs)
+        def _(d=d):
+            slab_copy(d, slab).wait_recv()
+            for l in range(lines):
+                for b in range(cells):
+                    weight[l * cells + b] *= jnp.broadcast_to(
+                        slab_in[d - 1, l][:, b : b + 1], tile
+                    )
+
     other_owners(lambda j, s: back_copy(j, me).wait_recv())
 
     def get(q):
@@ -334,10 +427,21 @@
                 scale = jnp.where(line[l] == e, factor[l], scale)
             updated[e, b] = conc[e, b] * scale
 
-    other_owners(lambda j, s: out_copy(j, s, me).wait_send())
+    @pl.when(slab < slabs - 1)
+    def _():
+        other_owners(lambda j, s: out_copy(j, s, me, cells).wait_send())
+
+    @pl.when(slab == slabs - 1)
+    def _():
+        other_owners(lambda j, s: out_copy(j, s, me, 1).wait_send())
+
     when(is_owner, lambda: other_bricks(lambda s: back_copy(rank, s).wait_send()))
     for d in range(1, slabs):
-        pl.when(slab >= d)(lambda d=d: slab_copy(d, slab - d).wait_send())
+
+        @pl.when(slab >= d)
+        def _(d=d):
+            loop(owners, lambda j: near_copy(d, j, slab - d, me).wait_send())
+            slab_copy(d, slab - d).wait_send()
 
 
 def per_device(
@@ -347,6 +451,7 @@
     lines = exit_mu.shape[0]
     owners, _, _, rows = layout(slices, bricks, lines)
     f32 = jnp.float32
+    others = max(slabs - 1, 1)
     arguments = (concentration, incident_mu, exit_mu, line_element, tilt_index, shear, data)
     return pl.pallas_call(
         functools.partial(kernel, bricks, slabs),
@@ -362,16 +467,20 @@
             pltpu.SMEM(tilt_index.shape, jnp.int32),
             pltpu.SMEM(shear.shape, jnp.int32),
             pltpu.VMEM((lines * cells, slices, width), f32),
-            pltpu.VMEM((slices, width), f32),
-            pltpu.VMEM((max(slabs - 1, 1), slices, width), f32),
+            pltpu.VMEM((lines, slices, width), f32),
+            pltpu.VMEM((others, lines, slices, width), f32),
             pltpu.VMEM((owners * rows, width), f32),
-            pltpu.VMEM((bricks, rows, width), f32),
+            pltpu.VMEM((others, bricks, rows, width), f32),
+            pltpu.VMEM((owners * cells * rows, width), f32),
+            pltpu.VMEM((bricks, cells * rows, width), f32),
             pltpu.VMEM((bricks, rows, width), f32),
             pltpu.VMEM((owners * rows, width), f32),
             pltpu.VMEM((owners * rows, width), f32),
             pltpu.SemaphoreType.DMA((7,)),
-            pltpu.SemaphoreType.DMA((max(slabs - 1, 1),)),
-            pltpu.SemaphoreType.DMA((max(slabs - 1, 1),)),
+            pltpu.SemaphoreType.DMA((others,)),
+            pltpu.SemaphoreType.DMA((others,)),
+            pltpu.SemaphoreType.DMA((others, owners)),
+            pltpu.SemaphoreType.DMA((others, bricks)),
             pltpu.SemaphoreType.DMA((owners,)),
             pltpu.SemaphoreType.DMA((bricks,)),
             pltpu.SemaphoreType.DMA((bricks,)),

time: 16.6 us -> 17.7 us (1.066)
  Pallas kernels: 15.1 us -> 16.2 us
    pallas_call x1, Pallas kernels: 15.1 us -> 16.2 us  [per_device(): pl.pallas_call(functools.partial(kernel, bricks, slabs), out_shape=pltpu....]
where the time goes in v3:
time: 17.7 us; the launch traced here: 17.6 us
  Pallas kernels  16.2 us (92%)
  local copies, waits for them, and re-layouts  0.71 us (4%)
  between operations  0.66 us (4%)
    pallas_call x1, Pallas kernels, per_device(): pl.pallas_call(functools.partial(kernel, bricks, slabs), out_shape=pltpu....  16.2 us
    unnamed x1, local copies, waits for them, and re-layouts  0.71 us

profile of v3, /device:TPU:0, one launch (start us, length us, event | category | flops | bytes accessed | tf_op | source)
XLA Modules:
  0.0 17.6 jit_solution(2433367240910914232)
XLA Ops:
  0.7 16.2 %update.1 = f32[8,4,16,128]{3,2,1,0:T(8,128)S(1)} custom-call(f32[8,4,16,128]{3,2,1,0:T(8,128)} %conc_hbm.1, f32[8]{0:T(128)} %incident_hbm.1, f32[3,8]{1,0:T(4,128)} %exit_hbm.1, s32[3]{0:T(128)} %line_hbm.1, s32[1]{0:T(128)S(6)} %copy.10.tilt_hbm, s32[16]{0:T(128)} %shear_hbm.1, f32[64,3,16,128]{3,2,1,0:T(8,128)} %data_hbm.1), custom_call_target="tpu_custom_call" | custom-call | tf_op jit(solution)/shard_map/update/pallas_call | solution.py:456
  16.9 0.7 %copy.9 = f32[8,4,16,128]{3,2,1,0:T(8,128)} copy(f32[8,4,16,128]{3,2,1,0:T(8,128)S(1)} %update.1) | data formatting | bytes 524288

commit v4 on v2

--- a/solution.py
+++ b/solution.py
@@ -108,7 +108,7 @@
 
     def other_bricks(body):
         if bricks <= 16:
-            for k in range(1, bricks):
+            for k in sorted(range(1, bricks), key=lambda k: abs(2 * k - bricks)):
                 body(lax.rem(me + k, bricks))
         else:
             loop(bricks, lambda s: pl.when(s != me)(lambda: body(s)))
@@ -241,27 +241,44 @@
         put(l + 1, partial)
 
     def part(j):
-        return pl.ds(pl.multiple_of(j * rows, 8), rows)
+        start = j * rows
+        return pl.ds(start if isinstance(j, int) else pl.multiple_of(start, 8), rows)
 
     def out_copy(j, target, source):
         return pltpu.make_async_remote_copy(
             src_ref=sent.at[part(j)],
-            dst_ref=taken.at[source],
-            send_sem=out_send.at[j],
-            recv_sem=out_recv.at[source],
+            dst_ref=taken.at[part(source)],
+            send_sem=out_send,
+            recv_sem=out_recv,
             device_id={"beam": target},
             device_id_type=MESH,
         )
 
     def back_copy(j, target):
         return pltpu.make_async_remote_copy(
-            src_ref=reply.at[target],
+            src_ref=reply.at[part(target)],
             dst_ref=back.at[part(j)],
-            send_sem=back_send.at[target],
-            recv_sem=back_recv.at[j],
+            send_sem=back_send,
+            recv_sem=back_recv,
             device_id={"beam": target},
             device_id_type=MESH,
         )
+
+    def all_of(ref, count, send_sem, recv_sem):
+        whole = ref.at[pl.ds(0, count * rows)]
+        return pltpu.make_async_remote_copy(
+            src_ref=whole,
+            dst_ref=whole,
+            send_sem=send_sem,
+            recv_sem=recv_sem,
+            device_id={"beam": lax.rem(me + 1, bricks)},
+            device_id_type=MESH,
+        )
+
+    def with_owners(body):
+        when(is_owner, lambda: body(owners - 1))
+        if stride > 1:
+            pl.when(jnp.logical_not(is_owner))(lambda: body(owners))
 
     other_owners(lambda j, s: out_copy(j, s, me).start())
 
@@ -276,8 +293,8 @@
         measured[pl.ds(r, owners, stride=rows), :] = jnp.zeros((owners, width), jnp.float32)
 
     def own():
-        taken[me] = sent[part(rank), :]
-        other_bricks(lambda s: out_copy(rank, s, s).wait_recv())
+        taken[part(me), :] = sent[part(rank), :]
+        all_of(taken, bricks - 1, out_send, out_recv).wait_recv()
         head = side((rows, width), 0) < chunk
 
         def one(s, carry):
@@ -287,8 +304,8 @@
             for q in range(1, lines + 1):
                 spread += pltpu.roll(start, q * chunk, 0)
             passed = jnp.exp(-spread)
-            reply[s] = passed
-            values = taken[s]
+            reply[part(s), :] = passed
+            values = taken[part(s), :]
             return run + values, emission + passed * values
 
         zero = jnp.zeros((rows, width), jnp.float32)
@@ -296,14 +313,14 @@
         ratio = measured[part(rank), :] / emission
 
         def finish(s):
-            reply[s] = jnp.where(head, reply[s], ratio)
+            reply[part(s), :] = jnp.where(head, reply[part(s), :], ratio)
 
         loop(bricks, finish)
         other_bricks(lambda s: back_copy(rank, s).start())
-        back[part(rank), :] = reply[me]
+        back[part(rank), :] = reply[part(me), :]
 
     when(is_owner, own)
-    other_owners(lambda j, s: back_copy(j, me).wait_recv())
+    with_owners(lambda count: all_of(back, count, back_send, back_recv).wait_recv())
 
     def get(q):
         return jnp.concatenate(
@@ -334,8 +351,8 @@
                 scale = jnp.where(line[l] == e, factor[l], scale)
             updated[e, b] = conc[e, b] * scale
 
-    other_owners(lambda j, s: out_copy(j, s, me).wait_send())
-    when(is_owner, lambda: other_bricks(lambda s: back_copy(rank, s).wait_send()))
+    with_owners(lambda count: all_of(sent, count, out_send, out_recv).wait_send())
+    when(is_owner, lambda: all_of(reply, bricks - 1, back_send, back_recv).wait_send())
     for d in range(1, slabs):
         pl.when(slab >= d)(lambda d=d: slab_copy(d, slab - d).wait_send())
 
@@ -365,17 +382,17 @@
             pltpu.VMEM((slices, width), f32),
             pltpu.VMEM((max(slabs - 1, 1), slices, width), f32),
             pltpu.VMEM((owners * rows, width), f32),
-            pltpu.VMEM((bricks, rows, width), f32),
-            pltpu.VMEM((bricks, rows, width), f32),
+            pltpu.VMEM((bricks * rows, width), f32),
+            pltpu.VMEM((bricks * rows, width), f32),
             pltpu.VMEM((owners * rows, width), f32),
             pltpu.VMEM((owners * rows, width), f32),
             pltpu.SemaphoreType.DMA((7,)),
             pltpu.SemaphoreType.DMA((max(slabs - 1, 1),)),
             pltpu.SemaphoreType.DMA((max(slabs - 1, 1),)),
-            pltpu.SemaphoreType.DMA((owners,)),
-            pltpu.SemaphoreType.DMA((bricks,)),
-            pltpu.SemaphoreType.DMA((bricks,)),
-            pltpu.SemaphoreType.DMA((owners,)),
+            pltpu.SemaphoreType.DMA,
+            pltpu.SemaphoreType.DMA,
+            pltpu.SemaphoreType.DMA,
+            pltpu.SemaphoreType.DMA,
         ],
         compiler_params=pltpu.CompilerParams(
             collective_id=0, has_side_effects=True, vmem_limit_bytes=16 * 1024 * 1024

time: 16.6 us -> 16.5 us (level)
  no operation moved by 1% of the time
where the time goes in v4:
time: 16.5 us; the launch traced here: 16.4 us
  Pallas kernels  15 us (91%)
  local copies, waits for them, and re-layouts  0.71 us (4%)
  between operations  0.66 us (4%)
    pallas_call x1, Pallas kernels, per_device(): pl.pallas_call(functools.partial(kernel, bricks, slabs), out_shape=pltpu....  15 us
    unnamed x1, local copies, waits for them, and re-layouts  0.71 us

profile of v4, /device:TPU:0, one launch (start us, length us, event | category | flops | bytes accessed | tf_op | source)
XLA Modules:
  0.0 16.4 jit_solution(6366437362040750636)
XLA Ops:
  0.7 15.0 %update.1 = f32[8,4,16,128]{3,2,1,0:T(8,128)S(1)} custom-call(f32[8,4,16,128]{3,2,1,0:T(8,128)} %conc_hbm.1, f32[8]{0:T(128)} %incident_hbm.1, f32[3,8]{1,0:T(4,128)} %exit_hbm.1, s32[3]{0:T(128)} %line_hbm.1, s32[1]{0:T(128)S(6)} %copy.10.tilt_hbm, s32[16]{0:T(128)} %shear_hbm.1, f32[64,3,16,128]{3,2,1,0:T(8,128)} %data_hbm.1), custom_call_target="tpu_custom_call" | custom-call | tf_op jit(solution)/shard_map/update/pallas_call | solution.py:368
  15.7 0.7 %copy.9 = f32[8,4,16,128]{3,2,1,0:T(8,128)} copy(f32[8,4,16,128]{3,2,1,0:T(8,128)S(1)} %update.1) | data formatting | bytes 524288

commit v5 on v4

--- a/solution.py
+++ b/solution.py
@@ -59,6 +59,7 @@
     line,
     tilt,
     shear,
+    sums,
     weight,
     slab_out,
     slab_in,
@@ -74,6 +75,7 @@
     out_recv,
     back_send,
     back_recv,
+    go,
 ):
     elements, cells, slices, width = conc.shape
     lines = exit_mu.shape[0]
@@ -97,7 +99,7 @@
             )
         )
     ]
-    for load in loads:
+    for load in loads[:-1]:
         load.start()
 
     def when(condition, body):
@@ -121,24 +123,34 @@
 
     barrier = pltpu.get_barrier_semaphore()
 
-    def greet_brick(s):
-        pl.semaphore_signal(barrier, inc=1, device_id={"beam": s}, device_id_type=MESH)
-
-    def greet_owner(j, s):
-        greet_brick(s)
+    def greet(brick, place):
+        pl.semaphore_signal(
+            barrier, inc=1, device_id={"beam": brick, "gy": place}, device_id_type=MESH
+        )
 
     for d in range(1, slabs):
-        pl.semaphore_signal(
-            barrier,
-            inc=1,
-            device_id={"gy": lax.rem(slab + d, slabs)},
-            device_id_type=MESH,
-        )
-    if stride == 1:
-        other_bricks(greet_brick)
-    else:
-        pl.when(is_owner)(lambda: other_bricks(greet_brick))
-        pl.when(jnp.logical_not(is_owner))(lambda: other_owners(greet_owner))
+        pl.when(slab + d < slabs)(lambda d=d: greet(me, slab + d))
+    pl.when(slab > 0)(lambda: greet(me, 0))
+
+    def greet_slab(body):
+        when(is_owner, lambda: other_bricks(lambda s: body(s)))
+        if stride > 1:
+            pl.when(jnp.logical_not(is_owner))(lambda: other_owners(lambda j, s: body(s)))
+
+    greet_slab(lambda s: greet(s, 0))
+
+    def first_slab():
+        when(
+            is_owner, lambda: pl.semaphore_wait(barrier, slabs * (bricks - 1) + slabs - 1)
+        )
+        if stride > 1:
+            pl.when(jnp.logical_not(is_owner))(
+                lambda: pl.semaphore_wait(barrier, slabs * owners + slabs - 1)
+            )
+        for d in range(1, slabs):
+            pl.semaphore_signal(
+                go, inc=1, device_id={"beam": me, "gy": slab + d}, device_id_type=MESH
+            )
 
     def side(shape, axis):
         return lax.broadcasted_iota(jnp.int32, shape, axis)
@@ -146,33 +158,38 @@
     square = (2 * width, 2 * width)
     row = lax.rem(side(square, 0), width)
     column = side(square, 1)
-    sums = jnp.where(
+    sums[...] = jnp.where(
         column >= width, 1.0, jnp.where(row > column, 1.0, jnp.where(row == column, 0.5, 0.0))
     ).astype(jnp.bfloat16)
 
     tile = (slices, width)
     z_of = side(tile, 0)
     lane = side(tile, 1)
-    for load in loads[:-1]:
+    for load in loads[1:-1]:
         load.wait()
+    mu = [[exit_mu[l, e] for e in range(elements)] for l in range(lines)]
+    mu_in = [incident_mu[e] for e in range(elements)]
+    emitter = [line[l] for l in range(lines)]
     first = jnp.zeros(tile, jnp.int32)
     for z in range(slices):
         first = jnp.where(z_of == z, shear[z], first)
     support = [
         jnp.where(me * cells + b >= first, 1.0, 0.0).astype(jnp.float32) for b in range(cells)
     ]
+    loads[0].wait()
+    loads[-1].start()
     exit_rate = []
     for l in range(lines):
         for b in range(cells):
-            total = conc[0, b] * exit_mu[l, 0]
+            total = conc[0, b] * mu[l][0]
             for e in range(1, elements):
-                total += conc[e, b] * exit_mu[l, e]
+                total += conc[e, b] * mu[l][e]
             exit_rate.append(total * support[b])
     stacked = jnp.concatenate(exit_rate, axis=0)
     high = stacked.astype(jnp.bfloat16)
     low = (stacked - high.astype(jnp.float32)).astype(jnp.bfloat16)
     paths = jnp.dot(
-        jnp.concatenate([high, low], axis=1), sums, preferred_element_type=jnp.float32
+        jnp.concatenate([high, low], axis=1), sums[...], preferred_element_type=jnp.float32
     )
 
     packed = jnp.zeros(tile, jnp.float32)
@@ -190,21 +207,16 @@
             device_id_type=MESH,
         )
 
-    if stride == 1:
-        pl.semaphore_wait(barrier, bricks - 1 + slabs - 1)
-    else:
-        pl.when(is_owner)(lambda: pl.semaphore_wait(barrier, bricks - 1 + slabs - 1))
-        pl.when(jnp.logical_not(is_owner))(
-            lambda: pl.semaphore_wait(barrier, owners + slabs - 1)
-        )
+    for g in range(1, slabs):
+        pl.when(slab == g)(lambda g=g: pl.semaphore_wait(barrier, g))
     for d in range(1, slabs):
         pl.when(slab >= d)(lambda d=d: slab_copy(d, slab - d).start())
 
     before = jnp.zeros(tile, jnp.float32)
     for b in range(cells):
-        rate = conc[0, b] * incident_mu[0]
+        rate = conc[0, b] * mu_in[0]
         for e in range(1, elements):
-            rate += conc[e, b] * incident_mu[e]
+            rate += conc[e, b] * mu_in[e]
         rate *= support[b]
         depth = before + 0.5 * rate
         before += rate
@@ -219,6 +231,7 @@
                 i * owners : (i + 1) * owners
             ]
 
+    pl.when(slab == 0)(first_slab)
     put(0, before)
     if rows > (lines + 1) * chunk:
         for r in range((lines + 1) * chunk, rows):
@@ -234,7 +247,7 @@
                 weight[c] *= jnp.broadcast_to(passed[:, c : c + 1], tile)
 
     for l in range(lines):
-        source = line[l]
+        source = emitter[l]
         partial = weight[l * cells] * conc[source, 0]
         for b in range(1, cells):
             partial += weight[l * cells + b] * conc[source, b]
@@ -280,6 +293,8 @@
         if stride > 1:
             pl.when(jnp.logical_not(is_owner))(lambda: body(owners))
 
+    if slabs > 1:
+        pl.when(slab > 0)(lambda: pl.semaphore_wait(go, 1))
     other_owners(lambda j, s: out_copy(j, s, me).start())
 
     loads[-1].wait()
@@ -330,9 +345,10 @@
     arrived = get(0)
     ratios = [get(l + 1) for l in range(lines)]
     same = [
-        [jnp.where(line[l] == line[k], 1.0, 0.0).astype(jnp.float32) for k in range(lines)]
+        [jnp.where(emitter[l] == emitter[k], 1.0, 0.0).astype(jnp.float32) for k in range(lines)]
         for l in range(lines)
     ]
+    hit = [[emitter[l] == e for e in range(elements)] for l in range(lines)]
     for b in range(cells):
         kept = [weight[l * cells + b] * arrived for l in range(lines)]
         raised = [kept[l] * ratios[l] for l in range(lines)]
@@ -348,7 +364,7 @@
         for e in range(elements):
             scale = 1.0
             for l in range(lines):
-                scale = jnp.where(line[l] == e, factor[l], scale)
+                scale = jnp.where(hit[l][e], factor[l], scale)
             updated[e, b] = conc[e, b] * scale
 
     with_owners(lambda count: all_of(sent, count, out_send, out_recv).wait_send())
@@ -378,6 +394,7 @@
             pltpu.SMEM(line_element.shape, jnp.int32),
             pltpu.SMEM(tilt_index.shape, jnp.int32),
             pltpu.SMEM(shear.shape, jnp.int32),
+            pltpu.VMEM((2 * width, 2 * width), jnp.bfloat16),
             pltpu.VMEM((lines * cells, slices, width), f32),
             pltpu.VMEM((slices, width), f32),
             pltpu.VMEM((max(slabs - 1, 1), slices, width), f32),
@@ -393,6 +410,7 @@
             pltpu.SemaphoreType.DMA,
             pltpu.SemaphoreType.DMA,
             pltpu.SemaphoreType.DMA,
+            pltpu.SemaphoreType.REGULAR,
         ],
         compiler_params=pltpu.CompilerParams(
             collective_id=0, has_side_effects=True, vmem_limit_bytes=16 * 1024 * 1024

time: 16.5 us -> 16.3 us (0.988)
  Pallas kernels: 15 us -> 14.8 us
    pallas_call x1, Pallas kernels: 15 us -> 14.8 us  [per_device(): pl.pallas_call(functools.partial(kernel, bricks, slabs), out_shape=pltpu....]
where the time goes in v5:
time: 16.3 us; the launch traced here: 16.2 us
  Pallas kernels  14.8 us (91%)
  local copies, waits for them, and re-layouts  0.71 us (4%)
  between operations  0.66 us (4%)
    pallas_call x1, Pallas kernels, per_device(): pl.pallas_call(functools.partial(kernel, bricks, slabs), out_shape=pltpu....  14.8 us
    unnamed x1, local copies, waits for them, and re-layouts  0.71 us

profile of v5, /device:TPU:0, one launch (start us, length us, event | category | flops | bytes accessed | tf_op | source)
XLA Modules:
  0.0 16.2 jit_solution(5882210229678445431)
XLA Ops:
  0.7 14.8 %update.1 = f32[8,4,16,128]{3,2,1,0:T(8,128)S(1)} custom-call(f32[8,4,16,128]{3,2,1,0:T(8,128)} %conc_hbm.1, f32[8]{0:T(128)} %incident_hbm.1, f32[3,8]{1,0:T(4,128)} %exit_hbm.1, s32[3]{0:T(128)} %line_hbm.1, s32[1]{0:T(128)S(6)} %copy.10.tilt_hbm, s32[16]{0:T(128)} %shear_hbm.1, f32[64,3,16,128]{3,2,1,0:T(8,128)} %data_hbm.1), custom_call_target="tpu_custom_call" | custom-call | tf_op jit(solution)/shard_map/update/pallas_call | solution.py:384
  15.5 0.7 %copy.9 = f32[8,4,16,128]{3,2,1,0:T(8,128)} copy(f32[8,4,16,128]{3,2,1,0:T(8,128)S(1)} %update.1) | data formatting | bytes 524288

commit v6 on v5

v6 whole, which is shorter than its diff:
```python
import functools

import jax
import jax.numpy as jnp
from jax import lax
from jax.experimental import pallas as pl
from jax.experimental.pallas import tpu as pltpu
from jax.sharding import PartitionSpec as P

blend_weight = 0.05
MESH = pl.DeviceIdType.MESH


def over(start, stop, body, carry=0):
    if stop - start <= 16:
        for step in range(start, stop):
            carry = body(step, carry)
        return carry
    return lax.fori_loop(start, stop, body, carry)


def kernel(
    bricks,
    slabs,
    conc_hbm,
    incident_hbm,
    exit_hbm,
    line_hbm,
    tilt_hbm,
    shear_hbm,
    data_hbm,
    updated,
    conc,
    data,
    incident_mu,
    exit_mu,
    line,
    tilt,
    shear,
    sums,
    weight,
    slab_out,
    slab_in,
    sent,
    taken,
    passed_out,
    passed_in,
    ratios,
    load_sem,
    slab_send,
    slab_recv,
    out_send,
    out_recv,
    passed_send,
    passed_recv,
    ratio_send,
    ratio_recv,
):
    elements, cells, slices, width = conc.shape
    lines = exit_mu.shape[0]
    me = lax.axis_index("beam")
    slab = lax.axis_index("gy")

    loads = [
        pltpu.make_async_copy(src, dst, load_sem.at[k])
        for k, (src, dst) in enumerate(
            (
                (conc_hbm, conc),
                (exit_hbm, exit_mu),
                (shear_hbm, shear),
                (incident_hbm, incident_mu),
                (line_hbm, line),
                (tilt_hbm, tilt),
                (data_hbm, data),
            )
        )
    ]
    for load in loads[:-1]:
        load.start()

    barrier = pltpu.get_barrier_semaphore()

    def greet(brick, place):
        pl.semaphore_signal(
            barrier, inc=1, device_id={"beam": brick, "gy": place}, device_id_type=MESH
        )

    for d in range(1, slabs):
        pl.when(slab + d < slabs)(lambda d=d: greet(me, slab + d))

    @pl.when(me == 0)
    def _():
        def one(n, carry):
            greet(n, slab)
            return carry

        over(1, bricks, one)
        loads[-1].start()

    pl.when(me > 0)(lambda: greet(0, slab))

    def side(shape, axis):
        return lax.broadcasted_iota(jnp.int32, shape, axis)

    square = (2 * width, 2 * width)
    row = lax.rem(side(square, 0), width)
    column = side(square, 1)
    sums[...] = jnp.where(
        column >= width, 1.0, jnp.where(row > column, 1.0, jnp.where(row == column, 0.5, 0.0))
    ).astype(jnp.bfloat16)

    tile = (slices, width)
    z_of = side(tile, 0)
    lane = side(tile, 1)
    for load in loads[1:-1]:
        load.wait()
    mu = [[exit_mu[l, e] for e in range(elements)] for l in range(lines)]
    mu_in = [incident_mu[e] for e in range(elements)]
    emitter = [line[l] for l in range(lines)]
    first = jnp.zeros(tile, jnp.int32)
    for z in range(slices):
        first = jnp.where(z_of == z, shear[z], first)
    support = [
        jnp.where(me * cells + b >= first, 1.0, 0.0).astype(jnp.float32) for b in range(cells)
    ]
    loads[0].wait()
    exit_rate = []
    for l in range(lines):
        for b in range(cells):
            total = conc[0, b] * mu[l][0]
            for e in range(1, elements):
                total += conc[e, b] * mu[l][e]
            exit_rate.append(total * support[b])
    stacked = jnp.concatenate(exit_rate, axis=0)
    high = stacked.astype(jnp.bfloat16)
    low = (stacked - high.astype(jnp.float32)).astype(jnp.bfloat16)
    paths = jnp.dot(
        jnp.concatenate([high, low], axis=1), sums[...], preferred_element_type=jnp.float32
    )

    packed = jnp.zeros(tile, jnp.float32)
    for c in range(lines * cells):
        packed = jnp.where(lane == c, paths[c * slices : (c + 1) * slices, width:], packed)
    slab_out[...] = packed

    def slab_copy(d, target):
        return pltpu.make_async_remote_copy(
            src_ref=slab_out,
            dst_ref=slab_in.at[d - 1],
            send_sem=slab_send.at[d - 1],
            recv_sem=slab_recv.at[d - 1],
            device_id={"gy": target},
            device_id_type=MESH,
        )

    pl.when(me == 0)(lambda: pl.semaphore_wait(barrier, bricks - 1 + slab))
    pl.when(me > 0)(lambda: pl.semaphore_wait(barrier, 1 + slab))
    for d in range(1, slabs):
        pl.when(slab >= d)(lambda d=d: slab_copy(d, slab - d).start())

    before = jnp.zeros(tile, jnp.float32)
    for b in range(cells):
        rate = conc[0, b] * mu_in[0]
        for e in range(1, elements):
            rate += conc[e, b] * mu_in[e]
        rate *= support[b]
        depth = before + 0.5 * rate
        before += rate
        for l in range(lines):
            c = l * cells + b
            path = paths[c * slices : (c + 1) * slices, :width]
            weight[c] = support[b] * jnp.exp(-(depth + path))

    sent[0] = before

    for d in range(1, slabs):

        @pl.when(slab + d < slabs)
        def _(d=d):
            slab_copy(d, slab).wait_recv()
            through = jnp.exp(-slab_in[d - 1])
            for c in range(lines * cells):
                weight[c] *= jnp.broadcast_to(through[:, c : c + 1], tile)

    for l in range(lines):
        partial = weight[l * cells] * conc[emitter[l], 0]
        for b in range(1, cells):
            partial += weight[l * cells + b] * conc[emitter[l], b]
        sent[l + 1] = partial

    def out_copy(n):
        return pltpu.make_async_remote_copy(
            src_ref=sent,
            dst_ref=taken.at[n],
            send_sem=out_send,
            recv_sem=out_recv.at[n],
            device_id={"beam": 0},
            device_id_type=MESH,
        )

    def passed_copy(n):
        return pltpu.make_async_remote_copy(
            src_ref=passed_out.at[n],
            dst_ref=passed_in,
            send_sem=passed_send.at[n],
            recv_sem=passed_recv,
            device_id={"beam": n},
            device_id_type=MESH,
        )

    def ratio_copy(n):
        return pltpu.make_async_remote_copy(
            src_ref=ratios,
            dst_ref=ratios,
            send_sem=ratio_send.at[n],
            recv_sem=ratio_recv,
            device_id={"beam": n},
            device_id_type=MESH,
        )

    @pl.when(me > 0)
    def _():
        out_copy(me).start()

    @pl.when(me == 0)
    def _():
        loads[-1].wait()

        def one(n, carry):
            run, emission = carry
            passed = jnp.exp(-run)
            passed_out[n] = passed
            passed_copy(n).start()
            out_copy(n).wait_recv()
            emission = tuple(
                emission[l] + passed * taken[n, l + 1] for l in range(lines)
            )
            return run + taken[n, 0], emission

        first_part = tuple(sent[l + 1] for l in range(lines))
        _, emission = over(1, bricks, one, (sent[0], first_part))
        for l in range(lines):
            ratios[l] = data[tilt[0], l] / emission[l]

        def reply(n, carry):
            ratio_copy(n).start()
            return carry

        over(1, bricks, reply)
        passed_in[...] = jnp.ones(tile, jnp.float32)

    same = [
        [jnp.where(emitter[l] == emitter[k], 1.0, 0.0).astype(jnp.float32) for k in range(lines)]
        for l in range(lines)
    ]
    hit = [[emitter[l] == e for e in range(elements)] for l in range(lines)]

    @pl.when(me > 0)
    def _():
        passed_copy(me).wait_recv()
        ratio_copy(me).wait_recv()

    arrived = passed_in[...]
    ratio = [ratios[l] for l in range(lines)]
    for b in range(cells):
        kept = [weight[l * cells + b] * arrived for l in range(lines)]
        raised = [kept[l] * ratio[l] for l in range(lines)]
        factor = []
        for l in range(lines):
            top = blend_weight + raised[l]
            bottom = blend_weight + kept[l]
            for k in range(lines):
                if k != l:
                    top += same[l][k] * raised[k]
                    bottom += same[l][k] * kept[k]
            factor.append(top / bottom)
        for e in range(elements):
            scale = 1.0
            for l in range(lines):
                scale = jnp.where(hit[l][e], factor[l], scale)
            updated[e, b] = conc[e, b] * scale

    @pl.when(me > 0)
    def _():
        out_copy(me).wait_send()

    @pl.when(me == 0)
    def _():
        def done(n, carry):
            passed_copy(n).wait_send()
            ratio_copy(n).wait_send()
            return carry

        over(1, bricks, done)

    for d in range(1, slabs):
        pl.when(slab >= d)(lambda d=d: slab_copy(d, slab - d).wait_send())


def per_device(
    bricks, slabs, concentration, incident_mu, exit_mu, line_element, tilt_index, shear, data
):
    elements, cells, slices, width = concentration.shape
    lines = exit_mu.shape[0]
    f32 = jnp.float32
    arguments = (concentration, incident_mu, exit_mu, line_element, tilt_index, shear, data)
    return pl.pallas_call(
        functools.partial(kernel, bricks, slabs),
        out_shape=pltpu.VMEM(concentration.shape, f32),
        in_specs=[pl.BlockSpec(memory_space=pl.ANY)] * 7,
        out_specs=pl.BlockSpec(memory_space=pltpu.VMEM),
        scratch_shapes=[
            pltpu.VMEM(concentration.shape, f32),
            pltpu.VMEM(data.shape, f32),
            pltpu.SMEM(incident_mu.shape, f32),
            pltpu.SMEM(exit_mu.shape, f32),
            pltpu.SMEM(line_element.shape, jnp.int32),
            pltpu.SMEM(tilt_index.shape, jnp.int32),
            pltpu.SMEM(shear.shape, jnp.int32),
            pltpu.VMEM((2 * width, 2 * width), jnp.bfloat16),
            pltpu.VMEM((lines * cells, slices, width), f32),
            pltpu.VMEM((slices, width), f32),
            pltpu.VMEM((max(slabs - 1, 1), slices, width), f32),
            pltpu.VMEM((lines + 1, slices, width), f32),
            pltpu.VMEM((bricks, lines + 1, slices, width), f32),
            pltpu.VMEM((bricks, slices, width), f32),
            pltpu.VMEM((slices, width), f32),
            pltpu.VMEM((lines, slices, width), f32),
            pltpu.SemaphoreType.DMA((7,)),
            pltpu.SemaphoreType.DMA((max(slabs - 1, 1),)),
            pltpu.SemaphoreType.DMA((max(slabs - 1, 1),)),
            pltpu.SemaphoreType.DMA,
            pltpu.SemaphoreType.DMA((bricks,)),
            pltpu.SemaphoreType.DMA((bricks,)),
            pltpu.SemaphoreType.DMA,
            pltpu.SemaphoreType.DMA((bricks,)),
            pltpu.SemaphoreType.DMA,
        ],
        compiler_params=pltpu.CompilerParams(
            collective_id=0, has_side_effects=True, vmem_limit_bytes=16 * 1024 * 1024
        ),
        name="update",
    )(*(x if x.size == 1 else pltpu.with_memory_space_constraint(x, pltpu.HBM) for x in arguments))


def solution(mesh):
    placed = (
        P("grp", "beam", None, "gy"),
        P(),
        P(),
        P(),
        P(),
        P("grp"),
        P("grp", None, None, "gy"),
    )
    return jax.shard_map(
        functools.partial(per_device, mesh.shape["beam"], mesh.shape["gy"]),
        mesh=mesh,
        in_specs=placed,
        out_specs=P("grp", "beam", None, "gy"),
        check_vma=False,
    )
```

time: 16.3 us -> 14.2 us (0.87)
  Pallas kernels: 14.8 us -> 12.7 us
    pallas_call x1, Pallas kernels: 14.8 us -> 12.7 us  [per_device(): pl.pallas_call(functools.partial(kernel, bricks, slabs), out_shape=pltpu....]
where the time goes in v6:
time: 14.2 us; the launch traced here: 14 us
  Pallas kernels  12.7 us (89%)
  local copies, waits for them, and re-layouts  0.71 us (5%)
  between operations  0.66 us (5%)
    pallas_call x1, Pallas kernels, per_device(): pl.pallas_call(functools.partial(kernel, bricks, slabs), out_shape=pltpu....  12.7 us
    unnamed x1, local copies, waits for them, and re-layouts  0.71 us

profile of v6, /device:TPU:0, one launch (start us, length us, event | category | flops | bytes accessed | tf_op | source)
XLA Modules:
  0.0 14.0 jit_solution(18946353655471923)
XLA Ops:
  0.7 12.7 %update.1 = f32[8,4,16,128]{3,2,1,0:T(8,128)S(1)} custom-call(f32[8,4,16,128]{3,2,1,0:T(8,128)} %conc_hbm.1, f32[8]{0:T(128)} %incident_hbm.1, f32[3,8]{1,0:T(4,128)} %exit_hbm.1, s32[3]{0:T(128)} %line_hbm.1, s32[1]{0:T(128)S(6)} %copy.10.tilt_hbm, s32[16]{0:T(128)} %shear_hbm.1, f32[64,3,16,128]{3,2,1,0:T(8,128)} %data_hbm.1), custom_call_target="tpu_custom_call" | custom-call | tf_op jit(solution)/shard_map/update/pallas_call | solution.py:307
  13.3 0.7 %copy.9 = f32[8,4,16,128]{3,2,1,0:T(8,128)} copy(f32[8,4,16,128]{3,2,1,0:T(8,128)S(1)} %update.1) | data formatting | bytes 524288

commit v7 on v6

--- a/solution.py
+++ b/solution.py
@@ -39,6 +39,10 @@
     shear,
     sums,
     weight,
+    light,
+    through,
+    total_out,
+    total_in,
     slab_out,
     slab_in,
     sent,
@@ -49,6 +53,8 @@
     load_sem,
     slab_send,
     slab_recv,
+    total_send,
+    total_recv,
     out_send,
     out_recv,
     passed_send,
@@ -134,13 +140,12 @@
     stacked = jnp.concatenate(exit_rate, axis=0)
     high = stacked.astype(jnp.bfloat16)
     low = (stacked - high.astype(jnp.float32)).astype(jnp.bfloat16)
-    paths = jnp.dot(
-        jnp.concatenate([high, low], axis=1), sums[...], preferred_element_type=jnp.float32
-    )
+    terms = jnp.concatenate([high, low], axis=1)
+    whole = jnp.dot(terms, sums[:, width:], preferred_element_type=jnp.float32)
 
     packed = jnp.zeros(tile, jnp.float32)
     for c in range(lines * cells):
-        packed = jnp.where(lane == c, paths[c * slices : (c + 1) * slices, width:], packed)
+        packed = jnp.where(lane == c, whole[c * slices : (c + 1) * slices], packed)
     slab_out[...] = packed
 
     def slab_copy(d, target):
@@ -158,35 +163,27 @@
     for d in range(1, slabs):
         pl.when(slab >= d)(lambda d=d: slab_copy(d, slab - d).start())
 
+    paths = jnp.dot(terms, sums[:, :width], preferred_element_type=jnp.float32)
     before = jnp.zeros(tile, jnp.float32)
+    depth = []
     for b in range(cells):
         rate = conc[0, b] * mu_in[0]
         for e in range(1, elements):
             rate += conc[e, b] * mu_in[e]
         rate *= support[b]
-        depth = before + 0.5 * rate
+        depth.append(before + 0.5 * rate)
         before += rate
-        for l in range(lines):
-            c = l * cells + b
-            path = paths[c * slices : (c + 1) * slices, :width]
-            weight[c] = support[b] * jnp.exp(-(depth + path))
-
-    sent[0] = before
-
-    for d in range(1, slabs):
-
-        @pl.when(slab + d < slabs)
-        def _(d=d):
-            slab_copy(d, slab).wait_recv()
-            through = jnp.exp(-slab_in[d - 1])
-            for c in range(lines * cells):
-                weight[c] *= jnp.broadcast_to(through[:, c : c + 1], tile)
-
-    for l in range(lines):
-        partial = weight[l * cells] * conc[emitter[l], 0]
-        for b in range(1, cells):
-            partial += weight[l * cells + b] * conc[emitter[l], b]
-        sent[l + 1] = partial
+    total_out[...] = before
+
+    def total_copy(n):
+        return pltpu.make_async_remote_copy(
+            src_ref=total_out,
+            dst_ref=total_in.at[n],
+            send_sem=total_send,
+            recv_sem=total_recv.at[n],
+            device_id={"beam": 0},
+            device_id_type=MESH,
+        )
 
     def out_copy(n):
         return pltpu.make_async_remote_copy(
@@ -198,6 +195,30 @@
             device_id_type=MESH,
         )
 
+    pl.when(me > 0)(lambda: total_copy(me).start())
+
+    for l in range(lines):
+        for b in range(cells):
+            c = l * cells + b
+            path = paths[c * slices : (c + 1) * slices]
+            weight[c] = support[b] * jnp.exp(-(depth[b] + path))
+            light[c] = weight[c] * conc[emitter[l], b]
+
+    for d in range(1, slabs):
+
+        @pl.when(slab + d < slabs)
+        def _(d=d):
+            slab_copy(d, slab).wait_recv()
+            through[d - 1] = jnp.exp(-slab_in[d - 1])
+            for c in range(lines * cells):
+                light[c] *= jnp.broadcast_to(through[d - 1][:, c : c + 1], tile)
+
+    for l in range(lines):
+        partial = light[l * cells]
+        for b in range(1, cells):
+            partial += light[l * cells + b]
+        sent[l] = partial
+
     def passed_copy(n):
         return pltpu.make_async_remote_copy(
             src_ref=passed_out.at[n],
@@ -218,36 +239,7 @@
             device_id_type=MESH,
         )
 
-    @pl.when(me > 0)
-    def _():
-        out_copy(me).start()
-
-    @pl.when(me == 0)
-    def _():
-        loads[-1].wait()
-
-        def one(n, carry):
-            run, emission = carry
-            passed = jnp.exp(-run)
-            passed_out[n] = passed
-            passed_copy(n).start()
-            out_copy(n).wait_recv()
-            emission = tuple(
-                emission[l] + passed * taken[n, l + 1] for l in range(lines)
-            )
-            return run + taken[n, 0], emission
-
-        first_part = tuple(sent[l + 1] for l in range(lines))
-        _, emission = over(1, bricks, one, (sent[0], first_part))
-        for l in range(lines):
-            ratios[l] = data[tilt[0], l] / emission[l]
-
-        def reply(n, carry):
-            ratio_copy(n).start()
-            return carry
-
-        over(1, bricks, reply)
-        passed_in[...] = jnp.ones(tile, jnp.float32)
+    pl.when(me > 0)(lambda: out_copy(me).start())
 
     same = [
         [jnp.where(emitter[l] == emitter[k], 1.0, 0.0).astype(jnp.float32) for k in range(lines)]
@@ -255,25 +247,69 @@
     ]
     hit = [[emitter[l] == e for e in range(elements)] for l in range(lines)]
 
-    @pl.when(me > 0)
+    for d in range(1, slabs):
+
+        @pl.when(slab + d < slabs)
+        def _(d=d):
+            for c in range(lines * cells):
+                weight[c] *= jnp.broadcast_to(through[d - 1][:, c : c + 1], tile)
+
+    def prepare():
+        arrived = passed_in[...]
+        for b in range(cells):
+            kept = [weight[l * cells + b] * arrived for l in range(lines)]
+            for l in range(lines):
+                bottom = blend_weight + kept[l]
+                for k in range(lines):
+                    if k != l:
+                        bottom += same[l][k] * kept[k]
+                weight[l * cells + b] = kept[l]
+                light[l * cells + b] = 1.0 / bottom
+
+    @pl.when(me == 0)
     def _():
-        passed_copy(me).wait_recv()
-        ratio_copy(me).wait_recv()
-
-    arrived = passed_in[...]
+        passed_in[...] = jnp.ones(tile, jnp.float32)
+
+    pl.when(me > 0)(lambda: passed_copy(me).wait_recv())
+    prepare()
+
+    @pl.when(me == 0)
+    def _():
+        loads[-1].wait()
+
+        def ahead(n, run):
+            passed_out[n] = jnp.exp(-run)
+            passed_copy(n).start()
+            total_copy(n).wait_recv()
+            return run + total_in[n]
+
+        over(1, bricks, ahead, total_out[...])
+
+        def one(n, emission):
+            out_copy(n).wait_recv()
+            return tuple(emission[l] + passed_out[n] * taken[n, l] for l in range(lines))
+
+        emission = over(1, bricks, one, tuple(sent[l] for l in range(lines)))
+        for l in range(lines):
+            ratios[l] = data[tilt[0], l] / emission[l]
+
+        def reply(n, carry):
+            ratio_copy(bricks - n).start()
+            return carry
+
+        over(1, bricks, reply)
+
+    pl.when(me > 0)(lambda: ratio_copy(me).wait_recv())
     ratio = [ratios[l] for l in range(lines)]
     for b in range(cells):
-        kept = [weight[l * cells + b] * arrived for l in range(lines)]
-        raised = [kept[l] * ratio[l] for l in range(lines)]
+        raised = [weight[l * cells + b] * ratio[l] for l in range(lines)]
         factor = []
         for l in range(lines):
             top = blend_weight + raised[l]
-            bottom = blend_weight + kept[l]
             for k in range(lines):
                 if k != l:
                     top += same[l][k] * raised[k]
-                    bottom += same[l][k] * kept[k]
-            factor.append(top / bottom)
+            factor.append(top * light[l * cells + b])
         for e in range(elements):
             scale = 1.0
             for l in range(lines):
@@ -282,6 +318,7 @@
 
     @pl.when(me > 0)
     def _():
+        total_copy(me).wait_send()
         out_copy(me).wait_send()
 
     @pl.when(me == 0)
@@ -319,16 +356,22 @@
             pltpu.SMEM(shear.shape, jnp.int32),
             pltpu.VMEM((2 * width, 2 * width), jnp.bfloat16),
             pltpu.VMEM((lines * cells, slices, width), f32),
+            pltpu.VMEM((lines * cells, slices, width), f32),
+            pltpu.VMEM((max(slabs - 1, 1), slices, width), f32),
+            pltpu.VMEM((slices, width), f32),
+            pltpu.VMEM((bricks, slices, width), f32),
             pltpu.VMEM((slices, width), f32),
             pltpu.VMEM((max(slabs - 1, 1), slices, width), f32),
-            pltpu.VMEM((lines + 1, slices, width), f32),
-            pltpu.VMEM((bricks, lines + 1, slices, width), f32),
+            pltpu.VMEM((lines, slices, width), f32),
+            pltpu.VMEM((bricks, lines, slices, width), f32),
             pltpu.VMEM((bricks, slices, width), f32),
             pltpu.VMEM((slices, width), f32),
             pltpu.VMEM((lines, slices, width), f32),
             pltpu.SemaphoreType.DMA((7,)),
             pltpu.SemaphoreType.DMA((max(slabs - 1, 1),)),
             pltpu.SemaphoreType.DMA((max(slabs - 1, 1),)),
+            pltpu.SemaphoreType.DMA,
+            pltpu.SemaphoreType.DMA((bricks,)),
             pltpu.SemaphoreType.DMA,
             pltpu.SemaphoreType.DMA((bricks,)),
             pltpu.SemaphoreType.DMA((bricks,)),

time: 14.2 us -> 14.2 us (level)
  no operation moved by 1% of the time
where the time goes in v7:
time: 14.2 us; the launch traced here: 14 us
  Pallas kernels  12.7 us (89%)
  local copies, waits for them, and re-layouts  0.71 us (5%)
  between operations  0.66 us (5%)
    pallas_call x1, Pallas kernels, per_device(): pl.pallas_call(functools.partial(kernel, bricks, slabs), out_shape=pltpu....  12.7 us
    unnamed x1, local copies, waits for them, and re-layouts  0.71 us

profile of v7, /device:TPU:0, one launch (start us, length us, event | category | flops | bytes accessed | tf_op | source)
XLA Modules:
  0.0 14.0 jit_solution(13741912424875157930)
XLA Ops:
  0.7 12.7 %update.1 = f32[8,4,16,128]{3,2,1,0:T(8,128)S(1)} custom-call(f32[8,4,16,128]{3,2,1,0:T(8,128)} %conc_hbm.1, f32[8]{0:T(128)} %incident_hbm.1, f32[3,8]{1,0:T(4,128)} %exit_hbm.1, s32[3]{0:T(128)} %line_hbm.1, s32[1]{0:T(128)S(6)} %copy.10.tilt_hbm, s32[16]{0:T(128)} %shear_hbm.1, f32[64,3,16,128]{3,2,1,0:T(8,128)} %data_hbm.1), custom_call_target="tpu_custom_call" | custom-call | tf_op jit(solution)/shard_map/update/pallas_call | solution.py:344
  13.3 0.7 %copy.9 = f32[8,4,16,128]{3,2,1,0:T(8,128)} copy(f32[8,4,16,128]{3,2,1,0:T(8,128)S(1)} %update.1) | data formatting | bytes 524288

commit v8 on v7

--- a/solution.py
+++ b/solution.py
@@ -103,7 +103,11 @@
         over(1, bricks, one)
         loads[-1].start()
 
+    even = lax.rem(me, 2) == 0
+    hands_on = jnp.logical_and(even, jnp.logical_and(me > 0, me + 1 < bricks))
+    plain = jnp.logical_and(me > 0, jnp.logical_not(hands_on))
     pl.when(me > 0)(lambda: greet(0, slab))
+    pl.when(jnp.logical_and(jnp.logical_not(even), me > 1))(lambda: greet(me - 1, slab))
 
     def side(shape, axis):
         return lax.broadcasted_iota(jnp.int32, shape, axis)
@@ -159,7 +163,8 @@
         )
 
     pl.when(me == 0)(lambda: pl.semaphore_wait(barrier, bricks - 1 + slab))
-    pl.when(me > 0)(lambda: pl.semaphore_wait(barrier, 1 + slab))
+    pl.when(hands_on)(lambda: pl.semaphore_wait(barrier, 2 + slab))
+    pl.when(plain)(lambda: pl.semaphore_wait(barrier, 1 + slab))
     for d in range(1, slabs):
         pl.when(slab >= d)(lambda d=d: slab_copy(d, slab - d).start())
 
@@ -293,13 +298,16 @@
         for l in range(lines):
             ratios[l] = data[tilt[0], l] / emission[l]
 
-        def reply(n, carry):
-            ratio_copy(bricks - n).start()
+        def reply(k, carry):
+            ratio_copy(2 * k).start()
             return carry
 
-        over(1, bricks, reply)
+        over(1, (bricks + 1) // 2, reply)
+        if bricks > 1:
+            ratio_copy(1).start()
 
     pl.when(me > 0)(lambda: ratio_copy(me).wait_recv())
+    pl.when(hands_on)(lambda: ratio_copy(me + 1).start())
     ratio = [ratios[l] for l in range(lines)]
     for b in range(cells):
         raised = [weight[l * cells + b] * ratio[l] for l in range(lines)]
@@ -325,10 +333,19 @@
     def _():
         def done(n, carry):
             passed_copy(n).wait_send()
-            ratio_copy(n).wait_send()
             return carry
 
         over(1, bricks, done)
+
+        def replied(k, carry):
+            ratio_copy(2 * k).wait_send()
+            return carry
+
+        over(1, (bricks + 1) // 2, replied)
+        if bricks > 1:
+            ratio_copy(1).wait_send()
+
+    pl.when(hands_on)(lambda: ratio_copy(me + 1).wait_send())
 
     for d in range(1, slabs):
         pl.when(slab >= d)(lambda d=d: slab_copy(d, slab - d).wait_send())

time: 14.2 us -> 15 us (1.056)
  the two profiles are of different devices: /device:TPU:0 before, /device:TPU:26 now
where the time goes in v8:
time: 15 us; the launch traced here: 14.9 us
  Pallas kernels  13.5 us (90%)
  local copies, waits for them, and re-layouts  0.71 us (5%)
  between operations  0.66 us (4%)
    pallas_call x1, Pallas kernels, per_device(): pl.pallas_call(functools.partial(kernel, bricks, slabs), out_shape=pltpu....  13.5 us
    unnamed x1, local copies, waits for them, and re-layouts  0.71 us

profile of v8, /device:TPU:26, one launch (start us, length us, event | category | flops | bytes accessed | tf_op | source)
XLA Modules:
  0.0 14.9 jit_solution(6849400950711114455)
XLA Ops:
  0.7 13.5 %update.1 = f32[8,4,16,128]{3,2,1,0:T(8,128)S(1)} custom-call(f32[8,4,16,128]{3,2,1,0:T(8,128)} %conc_hbm.1, f32[8]{0:T(128)} %incident_hbm.1, f32[3,8]{1,0:T(4,128)} %exit_hbm.1, s32[3]{0:T(128)} %line_hbm.1, s32[1]{0:T(128)S(6)} %copy.10.tilt_hbm, s32[16]{0:T(128)} %shear_hbm.1, f32[64,3,16,128]{3,2,1,0:T(8,128)} %data_hbm.1), custom_call_target="tpu_custom_call" | custom-call | tf_op jit(solution)/shard_map/update/pallas_call | solution.py:361
  14.2 0.7 %copy.9 = f32[8,4,16,128]{3,2,1,0:T(8,128)} copy(f32[8,4,16,128]{3,2,1,0:T(8,128)S(1)} %update.1) | data formatting | bytes 524288
